TPU v7x, 32 devices: a whole 2x2x4 slice. The times are simulated.
32 devices in a mesh: rep: 8 (over y, x, core), shard: 4 (over z).
Axes of the slice: x: 2, y: 2, z: 4, core: 2. Of those that a mesh axis runs over, the one named last changes fastest.
Arguments:
- tokens: bfloat16 [8192, 2048], P(('rep', 'shard')), may hold values from -6 to 6
- cotangent: bfloat16 [8192, 2048], P(('rep', 'shard')), may hold values from -6 to 6
- segment_ids: int32 [8192], P('rep'), may hold values from 0 to 4, as said below
- positions: int32 [8192], P(('rep', 'shard')), may hold values from 0 to 958, as said below
- projection_weight: float32 [2048, 3072], P(('shard', 'rep')), may hold values from -0.125 to 0.125
- projection_first_moment: float32 [2048, 3072], P(('shard', 'rep')), may hold values from -32 to 32
- projection_second_moment: float32 [2048, 3072], P(('shard', 'rep')), may hold values from 53.894737 to 431.1579
- out_weight: float32 [2048, 2048], P(None, ('shard', 'rep')), may hold values from -1 to 1
- out_first: float32 [2048, 2048], P(None, ('shard', 'rep')), may hold values from -6 to 6
- out_second: float32 [2048, 2048], P(None, ('shard', 'rep')), may hold values from 1.8947369 to 15.157895
- gate_up_weight: float32 [2048, 16384], P(('shard', 'rep')), may hold values from -0.125 to 0.125
- gate_up_first: float32 [2048, 16384], P(('shard', 'rep')), may hold values from -32 to 32
- gate_up_second: float32 [2048, 16384], P(('shard', 'rep')), may hold values from 53.894737 to 431.1579
- down_weight: float32 [8192, 2048], P(None, ('shard', 'rep')), may hold values from -0.0625 to 0.0625
- down_first: float32 [8192, 2048], P(None, ('shard', 'rep')), may hold values from -32 to 32
- down_second: float32 [8192, 2048], P(None, ('shard', 'rep')), may hold values from 77.60842 to 620.8674
- norm_gains: float32 [2, 2048], P(None, ('shard', 'rep')), may hold values from 0.5 to 1.5
- gains_first: float32 [2, 2048], P(None, ('shard', 'rep')), may hold values from -64 to 64
- gains_second: float32 [2, 2048], P(None, ('shard', 'rep')), may hold values from 215.57895 to 1724.6316
Outputs:
- layer_out: bfloat16 [8192, 2048], P(('rep', 'shard'))
- tokens_grad: bfloat16 [8192, 2048], P(('rep', 'shard'))
- qkv_first_new: float32 [2048, 3072], P(('shard', 'rep'))
- qkv_second_new: float32 [2048, 3072], P(('shard', 'rep'))
- qkv_weight_new: float32 [2048, 3072], P(('shard', 'rep'))
- out_first_new: float32 [2048, 2048], P(None, ('shard', 'rep'))
- out_second_new: float32 [2048, 2048], P(None, ('shard', 'rep'))
- out_weight_new: float32 [2048, 2048], P(None, ('shard', 'rep'))
- gate_up_first_new: float32 [2048, 16384], P(('shard', 'rep'))
- gate_up_second_new: float32 [2048, 16384], P(('shard', 'rep'))
- gate_up_weight_new: float32 [2048, 16384], P(('shard', 'rep'))
- down_first_new: float32 [8192, 2048], P(None, ('shard', 'rep'))
- down_second_new: float32 [8192, 2048], P(None, ('shard', 'rep'))
- down_weight_new: float32 [8192, 2048], P(None, ('shard', 'rep'))
- gains_first_new: float32 [2, 2048], P(None, ('shard', 'rep'))
- gains_second_new: float32 [2, 2048], P(None, ('shard', 'rep'))
- gains_new: float32 [2, 2048], P(None, ('shard', 'rep'))
Inputs may be any that keep to these rules, and one draw needn't show every extreme that they name: `segment_ids`: within each group of 1024 rows the segment numbers never fall, so segments are runs of consecutive rows; one segment of each group starts in the rows of the group's first device and ends in those of its last. `positions`: positions count up by one from 0 along each segment; the longest segment of each group has 959 rows.
All inputs are finite; a program needn't handle non-finite values.
Results may differ from a plain program's by a relative error of at most 0.025.
Values may be sent and summed in bfloat16 or wider, within the bound.
A program may use at most 1 GiB of HBM per device.

v0:
```python
import jax
import jax.numpy as jnp
from jax import lax
from jax.sharding import PartitionSpec as P

MODEL_WIDTH = 2048
QUERY_HEADS = 32
KEY_VALUE_HEADS = 8
HEAD_SIZE = 64
FF = 8192
STEP = 5


RATES = (0.05, 0.4, 0.05, 0.03, 1.0)
DECAYS = (0.1, 0.1, 0.1, 0.1, 0.0)


def to_bf(value):
    return value.astype(jnp.bfloat16)


def rms_scale(value):
    return lax.rsqrt(jnp.mean(value * value, axis=-1, keepdims=True) + 1e-05)


def tables(position_rows):
    freq = 500000.0 ** (-jnp.arange(HEAD_SIZE // 2, dtype=jnp.float32) * 2.0 / HEAD_SIZE)
    phase = position_rows.astype(jnp.float32)[:, None] * freq[None, :]
    phase = jnp.concatenate([phase, phase], axis=-1)
    return (jnp.cos(phase), jnp.sin(phase))


def rotate(flat, cos_table, sin_table, sign_value):
    num_rows = flat.shape[0]
    half_dim = HEAD_SIZE // 2
    heads = flat.reshape(num_rows, -1, HEAD_SIZE)
    turned = jnp.concatenate([-heads[..., half_dim:], heads[..., :half_dim]], axis=-1)
    return (heads * cos_table[:, None, :] + sign_value * turned * sin_table[:, None, :]).reshape(
        num_rows, -1
    )


def contract_last(left, right):
    return lax.dot_general(
        left, right, (((1,), (1,)), ((), ())), preferred_element_type=jnp.float32
    )


def outer_rows(left, right):
    return lax.dot_general(
        left, right, (((0,), (0,)), ((), ())), preferred_element_type=jnp.float32
    )


def norm_back(value, scale_rows, gain_row, grad_normed):
    weighted = grad_normed * gain_row
    inner = jnp.mean(value * weighted, axis=-1, keepdims=True)
    grad_in = scale_rows * weighted - value * scale_rows**3 * inner
    grad_gain = jnp.sum(value * scale_rows * grad_normed, axis=0)
    return (grad_in, grad_gain)


def adamw(weight, first, second, grad, rate, decay):
    first_new = 0.9 * first + 0.1 * grad
    second_new = 0.95 * second + 0.05 * grad * grad
    first_hat = first_new / (1.0 - 0.9**STEP)
    second_hat = second_new / (1.0 - 0.95**STEP)
    weight_new = weight - rate * (first_hat / (jnp.sqrt(second_hat) + 1e-08) + decay * weight)
    return (first_new, second_new, weight_new)


def on_device(
    tokens,
    cotangent,
    segment_ids,
    positions,
    projection_weight,
    projection_first_moment,
    projection_second_moment,
    out_weight,
    out_first,
    out_second,
    gate_up_weight,
    gate_up_first,
    gate_up_second,
    down_weight,
    down_first,
    down_second,
    norm_gains,
    gains_first,
    gains_second,
):
    shard_count = lax.axis_size("shard")
    rep_count = lax.axis_size("rep")
    shard_pos = lax.axis_index("shard")
    token_rows = tokens.shape[0]
    rows_of_group = segment_ids.shape[0]
    q_width = QUERY_HEADS * HEAD_SIZE
    key_value_width = KEY_VALUE_HEADS * HEAD_SIZE
    queries_per_key_head = QUERY_HEADS // KEY_VALUE_HEADS
    score_scale = HEAD_SIZE ** (-0.5)
    part_qkv, part_out, part_gu, part_down, part_gain = (
        lax.all_gather(to_bf(projection_weight), "rep", axis=0, tiled=True),
        lax.all_gather(to_bf(out_weight), "rep", axis=1, tiled=True),
        lax.all_gather(to_bf(gate_up_weight), "rep", axis=0, tiled=True),
        lax.all_gather(to_bf(down_weight), "rep", axis=1, tiled=True),
        lax.all_gather(to_bf(norm_gains), "rep", axis=1, tiled=True),
    )
    full_qkv, full_out, full_gu, full_down, full_gain = (
        lax.all_gather(part_qkv, "shard", axis=0, tiled=True),
        lax.all_gather(part_out, "shard", axis=1, tiled=True),
        lax.all_gather(part_gu, "shard", axis=0, tiled=True),
        lax.all_gather(part_down, "shard", axis=1, tiled=True),
        lax.all_gather(part_gain, "shard", axis=1, tiled=True),
    )
    gain_one = full_gain[0].astype(jnp.float32)
    gain_two = full_gain[1].astype(jnp.float32)
    tokens_f = tokens.astype(jnp.float32)
    scale_one = rms_scale(tokens_f)
    normed_one = to_bf(tokens_f * scale_one * gain_one)
    qkv_proj = jnp.dot(normed_one, full_qkv, preferred_element_type=jnp.float32)
    cos_table, sin_table = tables(positions)
    query_batch = to_bf(rotate(qkv_proj[:, :q_width], cos_table, sin_table, 1.0))
    key_b = to_bf(
        rotate(qkv_proj[:, q_width : q_width + key_value_width], cos_table, sin_table, 1.0)
    )
    value_b = to_bf(qkv_proj[:, q_width + key_value_width :])
    key_every_head, value_every_head = (
        lax.all_gather(key_b, "shard", axis=0, tiled=True),
        lax.all_gather(value_b, "shard", axis=0, tiled=True),
    )
    query_seg = lax.dynamic_slice_in_dim(segment_ids, shard_pos * token_rows, token_rows, 0)
    query_index = shard_pos * token_rows + jnp.arange(token_rows, dtype=jnp.int32)
    key_index = jnp.arange(rows_of_group, dtype=jnp.int32)
    allowed = (query_seg[:, None] == segment_ids[None, :]) & (
        key_index[None, :] <= query_index[:, None]
    )
    query_head_rows = query_batch.reshape(
        token_rows, KEY_VALUE_HEADS, queries_per_key_head, HEAD_SIZE
    ).transpose(1, 2, 0, 3)
    key_head_rows = key_every_head.reshape(rows_of_group, KEY_VALUE_HEADS, HEAD_SIZE).transpose(
        1, 0, 2
    )
    value_head_rows = value_every_head.reshape(rows_of_group, KEY_VALUE_HEADS, HEAD_SIZE).transpose(
        1, 0, 2
    )

    def masked_scores(q_one, k_one):
        scores = (
            jnp.einsum("gqd,kd->gqk", q_one, k_one, preferred_element_type=jnp.float32)
            * score_scale
        )
        return jnp.where(allowed[None], scores, -1e30)

    def head_forward(packed):
        q_one, k_one, v_one = packed
        scores = masked_scores(q_one, k_one)
        peak_score = jnp.max(scores, axis=-1, keepdims=True)
        exp_total = jnp.sum(jnp.exp(scores - peak_score), axis=-1, keepdims=True)
        log_sum = peak_score + jnp.log(exp_total)
        probs = to_bf(jnp.exp(scores - log_sum))
        attended = jnp.einsum("gqk,kd->gqd", probs, v_one, preferred_element_type=jnp.float32)
        return (attended, log_sum)

    attended, log_sums = lax.map(head_forward, (query_head_rows, key_head_rows, value_head_rows))
    out_b = to_bf(attended.transpose(2, 0, 1, 3).reshape(token_rows, q_width))
    hidden_one = tokens_f + jnp.dot(out_b, full_out, preferred_element_type=jnp.float32)
    scale_two = rms_scale(hidden_one)
    normed_two = to_bf(hidden_one * scale_two * gain_two)
    gate_up = jnp.dot(normed_two, full_gu, preferred_element_type=jnp.float32)
    gate_part = gate_up[:, :FF]
    up_part = gate_up[:, FF:]
    sigmoid_gate = jax.nn.sigmoid(gate_part)
    silu_gate = gate_part * sigmoid_gate
    hidden_b = to_bf(silu_gate * up_part)
    layer_out = to_bf(hidden_one + jnp.dot(hidden_b, full_down, preferred_element_type=jnp.float32))
    back_qkv, back_out, back_gu, back_down = (
        lax.all_gather(part_qkv, "shard", axis=0, tiled=True),
        lax.all_gather(part_out, "shard", axis=1, tiled=True),
        lax.all_gather(part_gu, "shard", axis=0, tiled=True),
        lax.all_gather(part_down, "shard", axis=1, tiled=True),
    )
    grad_hidden = contract_last(cotangent, back_down)
    grad_gate = grad_hidden * up_part * sigmoid_gate * (1.0 + gate_part * (1.0 - sigmoid_gate))
    grad_up = grad_hidden * silu_gate
    grad_gu_b = to_bf(jnp.concatenate([grad_gate, grad_up], axis=1))
    grad_normed_two = contract_last(grad_gu_b, back_gu)
    back_two, gain_two_grad = norm_back(hidden_one, scale_two, gain_two, grad_normed_two)
    grad_hidden_one = cotangent.astype(jnp.float32) + back_two
    grad_attn_b = to_bf(grad_hidden_one)
    output_grad_batch = to_bf(contract_last(grad_attn_b, back_out))
    output_grad_heads = output_grad_batch.reshape(
        token_rows, KEY_VALUE_HEADS, queries_per_key_head, HEAD_SIZE
    ).transpose(1, 2, 0, 3)

    def head_backward(packed):
        q_one, k_one, v_one, d_one, log_sum = packed
        probs = jnp.exp(masked_scores(q_one, k_one) - log_sum)
        grad_probs = jnp.einsum("gqd,kd->gqk", d_one, v_one, preferred_element_type=jnp.float32)
        inner = jnp.sum(grad_probs * probs, axis=-1, keepdims=True)
        grad_scores = to_bf(probs * (grad_probs - inner))
        grad_q = (
            jnp.einsum("gqk,kd->gqd", grad_scores, k_one, preferred_element_type=jnp.float32)
            * score_scale
        )
        grad_k = (
            jnp.einsum("gqk,gqd->kd", grad_scores, q_one, preferred_element_type=jnp.float32)
            * score_scale
        )
        grad_v = jnp.einsum("gqk,gqd->kd", to_bf(probs), d_one, preferred_element_type=jnp.float32)
        return (grad_q, grad_k, grad_v)

    grad_q, grad_k, grad_v = lax.map(
        head_backward,
        (query_head_rows, key_head_rows, value_head_rows, output_grad_heads, log_sums),
    )
    key_grad_all = grad_k.transpose(1, 0, 2).reshape(rows_of_group, key_value_width)
    value_grad_all = grad_v.transpose(1, 0, 2).reshape(rows_of_group, key_value_width)
    key_grad, value_grad = (
        lax.psum_scatter(
            key_grad_all.astype(jnp.bfloat16), "shard", scatter_dimension=0, tiled=True
        ).astype(jnp.float32),
        lax.psum_scatter(
            value_grad_all.astype(jnp.bfloat16), "shard", scatter_dimension=0, tiled=True
        ).astype(jnp.float32),
    )
    query_grad = grad_q.transpose(2, 0, 1, 3).reshape(token_rows, q_width)
    grad_qkv_b = to_bf(
        jnp.concatenate(
            [
                rotate(query_grad, cos_table, sin_table, -1.0),
                rotate(key_grad, cos_table, sin_table, -1.0),
                value_grad,
            ],
            axis=1,
        )
    )
    grad_normed_one = contract_last(grad_qkv_b, back_qkv)
    back_one, gain_one_grad = norm_back(tokens_f, scale_one, gain_one, grad_normed_one)
    tokens_grad = to_bf(grad_hidden_one + back_one)
    qkv_cols = q_width + 2 * key_value_width
    group_sums = lax.psum_scatter(
        jnp.concatenate(
            [
                outer_rows(normed_one, grad_qkv_b),
                outer_rows(grad_attn_b, out_b),
                outer_rows(normed_two, grad_gu_b),
                outer_rows(cotangent, hidden_b),
            ],
            axis=1,
        ).astype(jnp.bfloat16),
        "shard",
        scatter_dimension=0,
        tiled=True,
    )
    owner_sums = lax.psum_scatter(group_sums, "rep", scatter_dimension=0, tiled=True).astype(
        jnp.float32
    )
    grad_qkv_w = owner_sums[:, :qkv_cols]
    grad_out_w = owner_sums[:, qkv_cols : qkv_cols + q_width].T
    grad_gu_w = owner_sums[:, qkv_cols + q_width : qkv_cols + q_width + 2 * FF]
    grad_down_w = owner_sums[:, qkv_cols + q_width + 2 * FF :].T
    per_owner = MODEL_WIDTH // (shard_count * rep_count)
    gain_parts = jnp.stack([gain_one_grad, gain_two_grad])
    gain_parts = (
        gain_parts.reshape(2, shard_count, rep_count, per_owner)
        .transpose(0, 2, 1, 3)
        .reshape(2, MODEL_WIDTH)
    )
    grad_gain_w = lax.psum_scatter(gain_parts, ("rep", "shard"), scatter_dimension=1, tiled=True)
    new_qkv = adamw(
        projection_weight,
        projection_first_moment,
        projection_second_moment,
        grad_qkv_w,
        RATES[0],
        DECAYS[0],
    )
    new_out = adamw(out_weight, out_first, out_second, grad_out_w, RATES[1], DECAYS[1])
    new_gu = adamw(gate_up_weight, gate_up_first, gate_up_second, grad_gu_w, RATES[2], DECAYS[2])
    new_down = adamw(down_weight, down_first, down_second, grad_down_w, RATES[3], DECAYS[3])
    new_gain = adamw(norm_gains, gains_first, gains_second, grad_gain_w, RATES[4], DECAYS[4])
    return (
        layer_out,
        tokens_grad,
        new_qkv[0],
        new_qkv[1],
        new_qkv[2],
        new_out[0],
        new_out[1],
        new_out[2],
        new_gu[0],
        new_gu[1],
        new_gu[2],
        new_down[0],
        new_down[1],
        new_down[2],
        new_gain[0],
        new_gain[1],
        new_gain[2],
    )


def solution(mesh):
    in_specs = (
        P(("rep", "shard"), None),
        P(("rep", "shard"), None),
        P("rep"),
        P(("rep", "shard")),
        P(("shard", "rep"), None),
        P(("shard", "rep"), None),
        P(("shard", "rep"), None),
        P(None, ("shard", "rep")),
        P(None, ("shard", "rep")),
        P(None, ("shard", "rep")),
        P(("shard", "rep"), None),
        P(("shard", "rep"), None),
        P(("shard", "rep"), None),
        P(None, ("shard", "rep")),
        P(None, ("shard", "rep")),
        P(None, ("shard", "rep")),
        P(None, ("shard", "rep")),
        P(None, ("shard", "rep")),
        P(None, ("shard", "rep")),
    )
    out_specs = (
        P(("rep", "shard"), None),
        P(("rep", "shard"), None),
        P(("shard", "rep"), None),
        P(("shard", "rep"), None),
        P(("shard", "rep"), None),
        P(None, ("shard", "rep")),
        P(None, ("shard", "rep")),
        P(None, ("shard", "rep")),
        P(("shard", "rep"), None),
        P(("shard", "rep"), None),
        P(("shard", "rep"), None),
        P(None, ("shard", "rep")),
        P(None, ("shard", "rep")),
        P(None, ("shard", "rep")),
        P(None, ("shard", "rep")),
        P(None, ("shard", "rep")),
        P(None, ("shard", "rep")),
    )
    return jax.shard_map(
        on_device, mesh=mesh, in_specs=in_specs, out_specs=out_specs, check_vma=False
    )
```

profile of v0, /device:TPU:0, one launch (start us, length us, event | category | flops | bytes accessed | tf_op | source)
XLA Modules:
  0.0 4977.3 jit_solution(10984261362558233589)
XLA Ops:
  9.3 36.3 all-gather.12.cloned.1.call-done
  51.6 8.7 all-gather
  60.3 19.1 all_gather.41
  80.4 185.1 %all-gather.14.cloned.1.call-done = bf16[2048,3072]{1,0:T(8,128)(2,1)} async-done(((bf16[512,3072]{1,0:T(8,128)(2,1)}), bf16[2048,3072]{1,0:T(8,128)(2,1)}) %all-gather.14.cloned.1.call-update) | async-done | bytes 12582928 | tf_op jit(solution)/shard_map/all_gather | solution.py:110
  265.5 6.5 fusion.84
  279.1 14.9 all-gather.20.cloned.1.call-done
  294.1 92.1 %all-gather.24.cloned.1.call-done = bf16[512,16384]{1,0:T(8,128)(2,1)} async-done(((bf16[64,16384]{1,0:T(8,128)(2,1)}), bf16[512,16384]{1,0:T(8,128)(2,1)}) %all-gather.24.cloned.1.call-update) | async-done | bytes 16777232 | tf_op jit(solution)/shard_map/all_gather | solution.py:105
  386.3 56.7 %all-gather.28.cloned.1.call-done = bf16[8192,512]{0,1:T(8,128)(2,1)} async-done(((bf16[8192,64]{0,1:T(8,128)(2,1)}), bf16[8192,512]{0,1:T(8,128)(2,1)}) %all-gather.28.cloned.1.call-update) | async-done | bytes 8388624 | tf_op jit(solution)/shard_map/all_gather | solution.py:106
  462.4 10.6 all-gather.18.cloned.1.call-done
  475.2 27.3 all-gather.16.cloned.1.call-done
  504.8 44.8 while.30
  549.7 103.6 %all-gather.22.cloned.1.call-done = bf16[2048,2048]{0,1:T(8,128)(2,1)} async-done(((bf16[2048,512]{0,1:T(8,128)(2,1)}), bf16[2048,2048]{0,1:T(8,128)(2,1)}) %all-gather.22.cloned.1.call-update) | async-done | bytes 8388624 | tf_op jit(solution)/shard_map/all_gather | solution.py:111
  653.3 6.3 multiply_reduce_fusion.3
  659.6 1104.2 %all-gather.26.cloned.1.call-done = bf16[2048,16384]{1,0:T(8,128)(2,1)} async-done(((bf16[512,16384]{1,0:T(8,128)(2,1)}), bf16[2048,16384]{1,0:T(8,128)(2,1)}) %all-gather.26.cloned.1.call-update) | async-done | bytes 67108880 | tf_op jit(solution)/shard_map/all_gather | solution.py:112
  1763.8 39.1 fusion.93
  1802.9 521.9 %all-gather.30.cloned.1.call-done = bf16[8192,2048]{0,1:T(8,128)(2,1)} async-done(((bf16[8192,512]{0,1:T(8,128)(2,1)}), bf16[8192,2048]{0,1:T(8,128)(2,1)}) %all-gather.30.cloned.1.call-update) | async-done | bytes 33554448 | tf_op jit(solution)/shard_map/all_gather | solution.py:113
  2324.8 28.6 multiply_convert_fusion.2
  2353.4 30.0 multiply_reduce_fusion.1
  2386.6 7.4 convolution_convert_fusion.3
  2395.5 97.0 %while.31 = (s32[]{:T(128)}, f32[8,4,256,64]{2,3,1,0:T(8,128)}, bf16[8,1024,64]{1,2,0:T(8,128)(2,1)}, bf16[8,1024,64]{1,2,0:T(8,128)(2,1)}, bf16[8,4,256,64]{2,3...) while((s32[]{:T(128)}, f32[8,4,256,64]{2,3,1,0:T(8,128)}, ...), condition=%wide.region_9.10_spmd.clone.clone, body=%wide.region_7.9_spmd.clone.sunk.clone | while | flops 687733760 | bytes 34249856 | solution.py:213
  2492.6 29.3 convolution_convert_fusion
  2525.5 5.7 convolution_convert_fusion.2
  2531.2 12.4 copy.86
  2543.7 16.1 convert_bitcast_fusion
  2563.0 6.1 reduce-scatter.12.cloned.1.call-done
  2569.1 7.7 convolution_convert_fusion.1
  2576.8 79.3 %pad_maximum_fusion = bf16[2048,29696]{1,0:T(8,128)(2,1)} fusion(bf16[2048,8192]{1,0:T(8,128)(2,1)} %convert_bitcast_fusion, bf16[2048,16384]{1,0:T(8,128)(2,1)} %convolution_convert_fusion, bf16[2048,2048]{1,0:T(8,128)(2,1)} %copy.86, bf16[2048,3072]{1,0:T(8,128)(2,1)} %convolution_convert_fusion.1), kind=kLoop, calls=%fused_computation.66 | loop fusion | flops 486539264 | bytes 243269632 | tf_op jit(solution)/shard_map/concatenate | solution.py:243
  2657.1 10.4 fusion.67
  2669.1 1957.0 %reduce-scatter.18.cloned.1.call-done = bf16[512,29696]{1,0:T(8,128)(2,1)} async-done(((bf16[2048,29696]{1,0:T(8,128)(2,1)}), bf16[512,29696]{1,0:T(8,128)(2,1)}) %reduce-scatter.18.cloned.1.call-update) | async-done | bytes 30408720
  4626.1 17.5 fusion.63
  4646.8 119.8 %reduce-scatter.16.cloned.1.call-done = f32[64,2]{1,0:T(8,128)} async-done(((f32[2048,2]{1,0:T(8,128)}), f32[64,2]{1,0:T(8,128)}) %reduce-scatter.16.cloned.1.call-update) | async-done | bytes 528
  4768.0 182.8 %reduce-scatter.14.cloned.1.call-done = bf16[64,29696]{1,0:T(8,128)(2,1)} async-done(((bf16[512,29696]{1,0:T(8,128)(2,1)}), bf16[64,29696]{1,0:T(8,128)(2,1)}) %reduce-scatter.14.cloned.1.call-update) | async-done | bytes 3801104 | tf_op jit(solution)/shard_map/reduce_scatter | solution.py:256
  (292 shorter events, 219.7 us)
Async XLA Ops:
  7.2 38.4 copy-start.23
  7.2 38.3 all-gather.12.cloned.1.call-start
  9.2 256.2 %all-gather.14.cloned.1.call-start = ((), (), s32[]{:S(2)}) async-start(), calls=%async_computation.6 | async-start | bytes 15728640 | tf_op jit(solution)/shard_map/all_gather | solution.py:110
  45.6 248.5 %all-gather.20.cloned.1.call-start = ((), (), s32[]{:S(2)}) async-start(), calls=%async_computation.9 | async-start | bytes 2359296 | tf_op jit(solution)/shard_map/all_gather | solution.py:104
  46.4 339.9 %all-gather.24.cloned.1.call-start = ((), (), s32[]{:S(2)}) async-start(), calls=%async_computation.11 | async-start | bytes 18874368 | tf_op jit(solution)/shard_map/all_gather | solution.py:105
  50.3 29.2 copy-start.3
  50.3 392.7 %all-gather.28.cloned.1.call-start = ((), (), s32[]{:S(2)}) async-start(), calls=%async_computation.13 | async-start | bytes 9437184 | tf_op jit(solution)/shard_map/all_gather | solution.py:106
  51.5 421.5 %all-gather.18.cloned.1.call-start = ((), (), s32[]{:S(2)}) async-start(), calls=%async_computation.8 | async-start | bytes 1310720 | tf_op jit(solution)/shard_map/all_gather | solution.py:130
  80.3 191.7 %copy-start.36 = (f32[256]{0:T(256)}, f32[256]{0:T(256)S(1)}, u32[]{:S(2)}) copy-start(f32[256]{0:T(256)S(1)} %get-tuple-element.248) | copy-start | bytes 3076
  80.3 191.7 %copy-start.34 = (f32[1,2048]{1,0:T(1,128)}, f32[1,2048]{1,0:T(1,128)S(1)}, u32[]{:S(2)}) copy-start(f32[1,2048]{1,0:T(1,128)S(1)} %get-tuple-element.246) | copy-start | bytes 24580
  274.4 228.1 %all-gather.16.cloned.1.call-start = ((), (), s32[]{:S(2)}) async-start(), calls=%async_computation.7 | async-start | bytes 1310720 | tf_op jit(solution)/shard_map/all_gather | solution.py:129
  275.4 167.9 %copy-start.25 = (f32[256,64]{0,1:T(8,128)}, f32[256,64]{0,1:T(8,128)S(1)}, u32[]{:S(2)}) copy-start(f32[256,64]{0,1:T(8,128)S(1)} %get-tuple-element.244) | copy-start | bytes 196612
  279.1 374.2 %all-gather.22.cloned.1.call-start = ((), (), s32[]{:S(2)}) async-start(), calls=%async_computation.10 | async-start | bytes 10485760 | tf_op jit(solution)/shard_map/all_gather | solution.py:111
  294.1 1469.7 %all-gather.26.cloned.1.call-start = ((), (), s32[]{:S(2)}) async-start(), calls=%async_computation.12 | async-start | bytes 83886080 | tf_op jit(solution)/shard_map/all_gather | solution.py:112
  386.3 1938.5 %all-gather.30.cloned.1.call-start = ((), (), s32[]{:S(2)}) async-start(), calls=%async_computation.14 | async-start | bytes 41943040 | tf_op jit(solution)/shard_map/all_gather | solution.py:113
  443.0 2116.8 %reduce-scatter.10.cloned.1.call-start = ((), (), s32[]{:S(2)}) async-start(), calls=%async_computation.15 | async-start | bytes 1310720 | tf_op jit(solution)/shard_map/reduce_scatter | solution.py:220
  460.8 44.0 copy-start.11
  549.7 103.6 %copy-start.12 = (bf16[8,4,256,64]{2,3,1,0:T(8,128)(2,1)}, bf16[8,4,256,64]{2,3,1,0:T(8,128)(2,1)S(1)}, u32[]{:S(2)}) copy-start(bf16[8,4,256,64]{2,3,1,0:T(8,128)(2,1)S(1)} %get-tuple-element.109) | copy-start | bytes 3145732
  549.7 103.6 %copy-start.14 = (bf16[8,4,256,64]{2,3,1,0:T(8,128)(2,1)}, bf16[8,4,256,64]{2,3,1,0:T(8,128)(2,1)S(1)}, u32[]{:S(2)}) copy-start(bf16[8,4,256,64]{2,3,1,0:T(8,128)(2,1)S(1)} %get-tuple-element.536) | copy-start | bytes 3145732
  659.6 1693.9 %copy-start.6 = (f32[256,2048]{1,0:T(8,128)}, f32[256,2048]{1,0:T(8,128)S(1)}, u32[]{:S(2)}) copy-start(f32[256,2048]{1,0:T(8,128)S(1)} %get-tuple-element.252) | copy-start | bytes 6291460
  1763.8 561.0 %copy-start.17 = (bf16[256,2048]{1,0:T(8,128)(2,1)S(1)}, bf16[256,2048]{1,0:T(8,128)(2,1)}, u32[]{:S(2)}) copy-start(bf16[256,2048]{1,0:T(8,128)(2,1)} %param.24) | copy-start | bytes 3145732
  2386.6 138.9 %copy-start = (f32[256,2048]{1,0:T(8,128)}, f32[256,2048]{1,0:T(8,128)S(1)}, u32[]{:S(2)}) copy-start(f32[256,2048]{1,0:T(8,128)S(1)} %subtract_add_fusion) | copy-start | bytes 6291460
  2492.6 76.5 %reduce-scatter.12.cloned.1.call-start = ((), (), s32[]{:S(2)}) async-start(), calls=%async_computation.16 | async-start | bytes 1310720 | tf_op jit(solution)/shard_map/reduce_scatter | solution.py:223
  2543.6 2082.4 %reduce-scatter.18.cloned.1.call-start = ((), (), s32[]{:S(2)}) async-start(), calls=%async_computation.19 | async-start | bytes 152043520
  2543.7 25.4 copy-start.35
  2543.7 25.4 copy-start.37
  2656.2 2110.4 %reduce-scatter.16.cloned.1.call-start = ((), (), s32[]{:S(2)}) async-start(), calls=%async_computation.18 | async-start | bytes 1081344
  2669.0 2281.8 %reduce-scatter.14.cloned.1.call-start = ((), (), s32[]{:S(2)}) async-start(), calls=%async_computation.17 | async-start | bytes 34209792 | tf_op jit(solution)/shard_map/reduce_scatter | solution.py:256
  4643.6 123.8 %copy-start.41 = (f32[2,64]{1,0:T(2,128)S(1)}, f32[2,64]{1,0:T(2,128)}, u32[]{:S(2)}) copy-start(f32[2,64]{1,0:T(2,128)} %param.39) | copy-start | bytes 1540
  4643.6 123.8 %copy-start.42 = (f32[2,64]{1,0:T(2,128)S(1)}, f32[2,64]{1,0:T(2,128)}, u32[]{:S(2)}) copy-start(f32[2,64]{1,0:T(2,128)} %param.41) | copy-start | bytes 1540
  4643.6 123.8 %copy-start.43 = (f32[2,64]{1,0:T(2,128)S(1)}, f32[2,64]{1,0:T(2,128)}, u32[]{:S(2)}) copy-start(f32[2,64]{1,0:T(2,128)} %param.40) | copy-start | bytes 1540
  4768.0 185.5 %copy-start.24 = (f32[2048,64]{0,1:T(8,128)S(1)}, f32[2048,64]{0,1:T(8,128)}, u32[]{:S(2)}) copy-start(f32[2048,64]{0,1:T(8,128)} %param.30) | copy-start | bytes 1572868
  (29 other events, 148.8 us)
Sparse Core Ops, SparseCore 0:
  10.5 35.0 all-gather.11
  47.1 218.3 all-gather.13
  267.9 26.0 all-gather.19
  296.4 89.8 all-gather.23
  388.6 54.3 all-gather.27
  445.0 27.9 all-gather.17
  475.1 27.4 all-gather.15
  504.1 149.1 all-gather.21
  654.9 1108.8 all-gather.25
  1765.2 559.5 all-gather.29
  2492.7 25.3 reduce-scatter.9
  2543.7 25.3 reduce-scatter.11
  2656.3 1969.6 reduce-scatter.17
  4628.8 137.7 reduce-scatter.15
  4770.1 180.6 reduce-scatter.13
where the time goes:
time: 4980 us
  waiting for transfers between devices  4420 us (89%)
  matrix products  320 us (6%)
  other arithmetic  153 us (3%)
    unnamed x17, waiting for transfers between devices  2080 us
    all_gather x1, waiting for transfers between devices, on_device(): lax.all_gather(part_gu, 'shard', axis=0, tiled=True)  1100 us
    all_gather x1, waiting for transfers between devices, on_device(): lax.all_gather(part_down, 'shard', axis=1, tiled=True)  522 us
    all_gather x1, waiting for transfers between devices, on_device(): lax.all_gather(part_qkv, 'shard', axis=0, tiled=True)  185 us
    reduce_scatter x1, waiting for transfers between devices, on_device(): lax.psum_scatter(group_sums, 'rep', scatter_dimension=0, tiled=True)  183 us
    all_gather x1, waiting for transfers between devices, on_device(): lax.all_gather(part_out, 'shard', axis=1, tiled=True)  104 us
  transfers between devices with their start and end apart: 15, of which 14 were waited for; matrix products, arithmetic and copies ran while one was open for 5% of the time, Pallas kernels for 0%

commit v1 on v0

v1 whole, which is shorter than its diff:
```python
import functools

import jax
import jax.numpy as jnp
from jax import lax
from jax.experimental import pallas as pl
from jax.experimental.pallas import tpu as pltpu
from jax.sharding import PartitionSpec as P

MODEL_WIDTH = 2048
QUERY_HEADS = 32
KEY_VALUE_HEADS = 8
HEAD_SIZE = 64
FF = 8192
STEP = 5


RATES = (0.05, 0.4, 0.05, 0.03, 1.0)
DECAYS = (0.1, 0.1, 0.1, 0.1, 0.0)


def to_bf(value):
    return value.astype(jnp.bfloat16)


def to_f32(value):
    return value.astype(jnp.float32)


def rms_scale(value):
    return lax.rsqrt(jnp.mean(value * value, axis=-1, keepdims=True) + 1e-05)


def tables(position_rows):
    freq = 500000.0 ** (-jnp.arange(HEAD_SIZE // 2, dtype=jnp.float32) * 2.0 / HEAD_SIZE)
    phase = position_rows.astype(jnp.float32)[:, None] * freq[None, :]
    phase = jnp.concatenate([phase, phase], axis=-1)
    return (jnp.cos(phase), jnp.sin(phase))


def rotate(flat, cos_table, sin_table, sign_value):
    num_rows = flat.shape[0]
    half_dim = HEAD_SIZE // 2
    heads = flat.reshape(num_rows, -1, HEAD_SIZE)
    turned = jnp.concatenate([-heads[..., half_dim:], heads[..., :half_dim]], axis=-1)
    return (heads * cos_table[:, None, :] + sign_value * turned * sin_table[:, None, :]).reshape(
        num_rows, -1
    )


def dot(left, right):
    return jnp.dot(left, right, preferred_element_type=jnp.float32)


def contract_last(left, right):
    return lax.dot_general(
        left, right, (((1,), (1,)), ((), ())), preferred_element_type=jnp.float32
    )


def outer_rows(left, right):
    return lax.dot_general(
        left, right, (((0,), (0,)), ((), ())), preferred_element_type=jnp.float32
    )


def norm_back(value, scale_rows, gain_row, grad_normed):
    weighted = grad_normed * gain_row
    inner = jnp.mean(value * weighted, axis=-1, keepdims=True)
    return scale_rows * weighted - value * scale_rows**3 * inner


def adamw(weight, first, second, grad, rate, decay):
    first_new = 0.9 * first + 0.1 * grad
    second_new = 0.95 * second + 0.05 * grad * grad
    first_hat = first_new / (1.0 - 0.9**STEP)
    second_hat = second_new / (1.0 - 0.95**STEP)
    weight_new = weight - rate * (first_hat / (jnp.sqrt(second_hat) + 1e-08) + decay * weight)
    return (first_new, second_new, weight_new)


MESH = pl.DeviceIdType.MESH
VMEM_BYTES = 56 * 1024 * 1024


def after(value, *others):
    return lax.optimization_barrier((value, *others))[0]


def flipped(me, k):
    peer = me
    for bit in (1, 2, 4):
        mine = lax.rem(lax.div(me, jnp.int32(bit)), jnp.int32(2))
        if isinstance(k, int):
            on = (k // bit) % 2
            if not on:
                continue
        else:
            on = lax.rem(lax.div(k, jnp.int32(bit)), jnp.int32(2))
        peer = peer + on * bit * (1 - 2 * mine)
    return peer


def call_peers(peers):
    barrier = pltpu.get_barrier_semaphore()
    for peer in peers:
        pl.semaphore_signal(barrier, inc=1, device_id={"rep": peer}, device_id_type=MESH)


def await_peers(peers):
    pl.semaphore_wait(pltpu.get_barrier_semaphore(), len(peers))


def remote(src, dst, sems, index, peer):
    return pltpu.make_async_remote_copy(
        src_ref=src,
        dst_ref=dst,
        send_sem=sems[0].at[index],
        recv_sem=sems[1].at[index],
        device_id={"rep": peer},
        device_id_type=MESH,
    )


def swap_halves(value):
    return pltpu.roll(value, HEAD_SIZE, axis=1)


def head_at(rows, head, low_half):
    pair = to_f32(rows[:, (head // 2) * 128 : (head // 2) * 128 + 128])
    if (head % 2 == 0) != low_half:
        pair = swap_halves(pair)
    lane = lax.broadcasted_iota(jnp.int32, pair.shape, 1)
    keep = lane < HEAD_SIZE if low_half else lane >= HEAD_SIZE
    return to_bf(jnp.where(keep, pair, 0.0))


def joined(even, odd, low_half):
    lane = lax.broadcasted_iota(jnp.int32, even.shape, 1)
    if low_half:
        return jnp.where(lane < HEAD_SIZE, even, swap_halves(odd))
    return jnp.where(lane < HEAD_SIZE, swap_halves(even), odd)


def lower_keys(kv_ref):
    lines, rows, wide = kv_ref.shape
    kv = to_f32(kv_ref[...].reshape(lines * rows, wide))
    came = lax.broadcasted_iota(jnp.int32, kv.shape, 0) < (lax.axis_index("shard") + 1) * rows
    return to_bf(jnp.where(came, kv, 0.0))


def turned_pair(both):
    lane = lax.broadcasted_iota(jnp.int32, both.shape, 1)
    low = lax.rem(lane, jnp.int32(HEAD_SIZE)) < HEAD_SIZE // 2
    back = pltpu.roll(both, 128 - HEAD_SIZE // 2, axis=1)
    return jnp.where(low, -back, pltpu.roll(both, HEAD_SIZE // 2, axis=1))


def angle_pair(table):
    count = HEAD_SIZE // 2
    return [
        jnp.concatenate([table[:, at : at + count]] * 4, axis=1) for at in (0, count)
    ]


def project_kernel(x_ref, w_ref, gain_ref, table_ref, normed_ref, q_ref, kv_ref):
    x = to_f32(x_ref[0])
    normed = to_bf(x * rms_scale(x) * gain_ref[...])
    normed_ref[0] = normed
    qkv = dot(normed, w_ref[...])
    cos_pair, sin_pair = angle_pair(table_ref[0])

    def turn(pair):
        return pair * cos_pair + turned_pair(pair) * sin_pair

    for pair in range(2):
        at = slice(pair * 128, pair * 128 + 128)
        q_ref[:, at] = to_bf(to_f32(to_bf(turn(qkv[:, at]))) * HEAD_SIZE**-0.5)
    key_value = qkv[:, 256:384]
    lane = lax.broadcasted_iota(jnp.int32, key_value.shape, 1)
    kv_ref[...] = to_bf(jnp.where(lane < HEAD_SIZE, turn(key_value), key_value))


def project(tokens_all, weights, gain, table):
    _, rows, depth = tokens_all.shape
    bf = jnp.bfloat16
    return pl.pallas_call(
        project_kernel,
        grid=(8,),
        in_specs=[
            pl.BlockSpec((1, rows, depth), lambda i: (i, 0, 0)),
            pl.BlockSpec((depth, 384), lambda i: (0, 0)),
            pl.BlockSpec((1, depth), lambda i: (0, 0)),
            pl.BlockSpec((1, rows, 128), lambda i: (i, 0, 0)),
        ],
        out_specs=[
            pl.BlockSpec((1, rows, depth), lambda i: (i, 0, 0)),
            pl.BlockSpec((rows, 256), lambda i: (i, 0)),
            pl.BlockSpec((rows, 128), lambda i: (i, 0)),
        ],
        out_shape=[
            jax.ShapeDtypeStruct((8, rows, depth), bf),
            jax.ShapeDtypeStruct((8 * rows, 256), bf),
            jax.ShapeDtypeStruct((8 * rows, 128), bf),
        ],
        compiler_params=pltpu.CompilerParams(vmem_limit_bytes=VMEM_BYTES),
        name="project",
    )(tokens_all, weights, gain, table)


def attend_kernel(q_ref, kv_ref, seg_q_ref, seg_k_ref, own_ref, log_ref, sent_ref, out_buf, send, recv, local):
    step = pl.program_id(0)
    slot = 7 - step
    me = lax.axis_index("rep")
    peers = [flipped(me, k) for k in range(1, 8)]
    rows = q_ref.shape[0]
    keys = kv_ref.shape[0] * kv_ref.shape[1]

    @pl.when(step == 0)
    def _():
        call_peers(peers)

    kv = lower_keys(kv_ref)
    row_at = lax.axis_index("shard") * rows + lax.broadcasted_iota(jnp.int32, (rows, keys), 0)
    key_at = lax.broadcasted_iota(jnp.int32, (rows, keys), 1)
    allowed = (seg_q_ref[0] == seg_k_ref[0]) & (key_at <= row_at)
    bias = jnp.where(allowed, 0.0, -1e30)
    q = q_ref[...]
    outs = []
    for head in range(4):
        scores = contract_last(head_at(q, head, True), kv) + bias
        peak = jnp.max(scores, axis=1, keepdims=True)
        probs = jnp.exp(scores - peak)
        total = jnp.sum(probs, axis=1, keepdims=True)
        log_ref[0, :, head : head + 1] = peak + jnp.log(total)
        outs.append(dot(to_bf(probs), kv) * (1.0 / total))
    for pair in range(2):
        out_buf[slot, :, pair * 128 : pair * 128 + 128] = to_bf(
            joined(outs[2 * pair], outs[2 * pair + 1], False)
        )
    own_ref[...] = out_buf[slot]

    @pl.when(step == 0)
    def _():
        await_peers(peers)

    def copy(k):
        place = sent_ref.at[:, pl.ds(pl.multiple_of(k * 256, 256), 256)]
        return remote(out_buf.at[k], place, (send, recv), k, flipped(me, k))

    @pl.when(slot > 0)
    def _():
        copy(slot).start()

    @pl.when(slot == 0)
    def _():
        mine = pltpu.make_async_copy(out_buf.at[0], sent_ref.at[:, pl.ds(0, 256)], local)
        mine.start()
        for k in range(1, 8):
            copy(k).wait()
        mine.wait()


def attend(q, kv_line, seg_q, seg_k):
    lines, plane, _ = kv_line.shape
    rows = plane // 8
    return pl.pallas_call(
        attend_kernel,
        grid=(8,),
        in_specs=[
            pl.BlockSpec((rows, 256), lambda i: (7 - i, 0)),
            pl.BlockSpec((lines, rows, 128), lambda i: (0, 7 - i, 0)),
            pl.BlockSpec((1, rows, 1), lambda i: (7 - i, 0, 0)),
            pl.BlockSpec((1, 1, lines * rows), lambda i: (7 - i, 0, 0)),
        ],
        out_specs=[
            pl.BlockSpec((rows, 256), lambda i: (7 - i, 0)),
            pl.BlockSpec((1, rows, 4), lambda i: (7 - i, 0, 0)),
            pl.BlockSpec(memory_space=pl.ANY),
        ],
        out_shape=[
            jax.ShapeDtypeStruct((plane, 256), jnp.bfloat16),
            jax.ShapeDtypeStruct((8, rows, 4), jnp.float32),
            jax.ShapeDtypeStruct((rows, 2048), jnp.bfloat16),
        ],
        scratch_shapes=[
            pltpu.VMEM((8, rows, 256), jnp.bfloat16),
            pltpu.SemaphoreType.DMA((8,)),
            pltpu.SemaphoreType.DMA((8,)),
            pltpu.SemaphoreType.DMA,
        ],
        compiler_params=pltpu.CompilerParams(
            collective_id=1, has_side_effects=True, vmem_limit_bytes=VMEM_BYTES
        ),
        name="attend",
    )(q, kv_line, seg_q, seg_k)


def attend_back_kernel(
    d_ref, q_ref, kv_ref, seg_q_ref, seg_k_ref, log_ref, table_ref, block_ref,
    dq_ref, dkv_ref, blocks_ref,
    d_buf, send, recv, local, block_send, block_recv, block_local,
):
    slot = pl.program_id(0)
    me = lax.axis_index("rep")
    peers = [flipped(me, k) for k in range(1, 8)]
    rows = q_ref.shape[0]
    lines = kv_ref.shape[0]
    keys = lines * kv_ref.shape[1]

    def copy(k):
        piece = d_ref.at[:, pl.ds(pl.multiple_of(k * 256, 256), 256)]
        return remote(piece, d_buf.at[k], (send, recv), k, flipped(me, k))

    spread = Spread(
        me, block_ref, lambda k: blocks_ref.at[k], (block_send, block_recv), block_local
    )

    @pl.when(slot == 0)
    def _():
        call_peers(peers)
        mine = pltpu.make_async_copy(d_ref.at[:, pl.ds(0, 256)], d_buf.at[0], local)
        mine.start()
        await_peers(peers)
        for k in range(1, 8):
            copy(k).start()
        spread.begin()
        mine.wait()

    @pl.when(slot > 0)
    def _():
        copy(slot).wait_recv()

    @pl.when(slot == 5)
    def _():
        spread.middle()

    kv = lower_keys(kv_ref)
    key_at = lax.broadcasted_iota(jnp.int32, (keys, rows), 0)
    row_at = lax.axis_index("shard") * rows + lax.broadcasted_iota(jnp.int32, (keys, rows), 1)
    allowed = (seg_k_ref[0] == seg_q_ref[0]) & (key_at <= row_at)
    bias = jnp.where(allowed, 0.0, -1e30)
    q = q_ref[...]
    d_out = d_buf[slot]
    grads = []
    dkv = jnp.zeros((keys, 128), jnp.float32)
    for head in range(4):
        q_one = head_at(q, head, True)
        d_one = head_at(d_out, head, False)
        probs = jnp.exp(contract_last(kv, q_one) + bias - log_ref[0, head : head + 1, :])
        grad_probs = contract_last(kv, d_one)
        inner = jnp.sum(grad_probs * probs, axis=0, keepdims=True)
        grad_scores = to_bf(probs * (grad_probs - inner))
        grads.append(outer_rows(grad_scores, kv))
        dkv = dkv + dot(grad_scores, q_one) + dot(to_bf(probs), d_one)
    cos_pair, sin_pair = angle_pair(table_ref[0])
    for pair in range(2):
        both = joined(grads[2 * pair], grads[2 * pair + 1], True) * (HEAD_SIZE**-0.5)
        dq_ref[:, pair * 128 : pair * 128 + 128] = to_bf(
            both * cos_pair - turned_pair(both) * sin_pair
        )
    dkv_ref[...] = to_bf(dkv).reshape(lines, rows, 128)

    @pl.when(slot == 7)
    def _():
        for k in range(1, 8):
            copy(k).wait_send()
        spread.last()
        spread.end()


def attend_back(d_own, block, q, kv_line, seg_q, seg_k, logs, table):
    lines, plane, _ = kv_line.shape
    rows = plane // 8
    bf = jnp.bfloat16
    return pl.pallas_call(
        attend_back_kernel,
        grid=(8,),
        in_specs=[
            pl.BlockSpec(memory_space=pl.ANY),
            pl.BlockSpec((rows, 256), lambda i: (i, 0)),
            pl.BlockSpec((lines, rows, 128), lambda i: (0, i, 0)),
            pl.BlockSpec((1, 1, rows), lambda i: (i, 0, 0)),
            pl.BlockSpec((1, lines * rows, 1), lambda i: (i, 0, 0)),
            pl.BlockSpec((1, 4, rows), lambda i: (i, 0, 0)),
            pl.BlockSpec((1, rows, 128), lambda i: (i, 0, 0)),
            pl.BlockSpec(memory_space=pl.ANY),
        ],
        out_specs=[
            pl.BlockSpec((rows, 256), lambda i: (i, 0)),
            pl.BlockSpec((lines, rows, 128), lambda i: (0, i, 0)),
            pl.BlockSpec(memory_space=pl.ANY),
        ],
        out_shape=[
            jax.ShapeDtypeStruct((plane, 256), bf),
            jax.ShapeDtypeStruct((lines, plane, 128), bf),
            jax.ShapeDtypeStruct((8, *block.shape), block.dtype),
        ],
        scratch_shapes=[
            pltpu.VMEM((8, rows, 256), bf),
            pltpu.SemaphoreType.DMA((8,)),
            pltpu.SemaphoreType.DMA((8,)),
            pltpu.SemaphoreType.DMA,
            pltpu.SemaphoreType.DMA((7,)),
            pltpu.SemaphoreType.DMA((7,)),
            pltpu.SemaphoreType.DMA,
        ],
        compiler_params=pltpu.CompilerParams(
            collective_id=2, has_side_effects=True, vmem_limit_bytes=VMEM_BYTES
        ),
        name="attend_back",
    )(d_own, q, kv_line, seg_q, seg_k, logs, table, block)


def corner_route(me):
    core = lax.rem(me, jnp.int32(2))
    first, second = 2 + 2 * core, 4 - 2 * core
    return first, second, flipped(me, 1), flipped(me, first), flipped(me, second)


class Spread:
    def __init__(self, me, source, place, sems, local):
        first, second, sibling, one, two = corner_route(me)
        self.own = lambda: pltpu.make_async_copy(source, place(0), local)
        self.to_sibling = lambda: remote(source, place(1), sems, 0, sibling)
        self.to_one = lambda: remote(source, place(first), sems, 1, one)
        self.to_two = lambda: remote(source, place(second), sems, 2, two)
        self.corner = lambda: remote(place(second), place(6), sems, 3, one)
        self.pass_first = lambda: remote(place(first), place(first + 1), sems, 4, sibling)
        self.pass_second = lambda: remote(place(second), place(second + 1), sems, 5, sibling)
        self.pass_corner = lambda: remote(place(6), place(7), sems, 6, sibling)

    def begin(self):
        self.own().start()
        self.to_one().start()
        self.to_two().start()
        self.to_sibling().start()

    def middle(self):
        self.to_two().wait_recv()
        self.corner().start()
        self.pass_second().start()
        self.to_one().wait_recv()
        self.pass_first().start()

    def last(self):
        self.corner().wait_recv()
        self.pass_corner().start()

    def end(self):
        for move in (self.to_sibling, self.pass_first, self.pass_second, self.pass_corner):
            move().wait_recv()
        for move in (
            self.to_one,
            self.to_two,
            self.to_sibling,
            self.corner,
            self.pass_first,
            self.pass_second,
            self.pass_corner,
        ):
            move().wait_send()
        self.own().wait()


def gather_kernel(columns, *refs):
    count = len(columns)
    sources, outs = refs[:count], refs[count : 2 * count]
    send, recv, local = refs[2 * count :]
    me = lax.axis_index("rep")
    peers = [flipped(me, k) for k in (1, 2, 4)]
    call_peers(peers)

    def spread(i):
        source = sources[i]
        if columns[i] is None:
            return Spread(me, source, lambda k: outs[i].at[k], (send.at[i], recv.at[i]), local.at[i])
        start, width = columns[i]

        def place(k):
            return outs[i].at[:, pl.ds(pl.multiple_of(k * width, width), width)]

        source = source.at[:, pl.ds(start, width)]
        return Spread(me, source, place, (send.at[i], recv.at[i]), local.at[i])

    spreads = [spread(i) for i in range(count)]
    await_peers(peers)
    for one in spreads:
        one.begin()
    for one in spreads:
        one.middle()
    for one in spreads:
        one.last()
    for one in spreads:
        one.end()


def plane_gather(blocks, columns, number):
    count = len(blocks)
    shapes = [
        (8, *b.shape) if c is None else (b.shape[0], 8 * c[1]) for b, c in zip(blocks, columns)
    ]
    return pl.pallas_call(
        functools.partial(gather_kernel, columns),
        in_specs=[pl.BlockSpec(memory_space=pl.ANY)] * count,
        out_specs=[pl.BlockSpec(memory_space=pl.ANY)] * count,
        out_shape=[jax.ShapeDtypeStruct(s, b.dtype) for s, b in zip(shapes, blocks)],
        scratch_shapes=[
            pltpu.SemaphoreType.DMA((count, 7)),
            pltpu.SemaphoreType.DMA((count, 7)),
            pltpu.SemaphoreType.DMA((count,)),
        ],
        compiler_params=pltpu.CompilerParams(collective_id=number, has_side_effects=True),
        name=f"plane_gather_{number}",
    )(*blocks)


def call_line(line, count):
    barrier = pltpu.get_barrier_semaphore()
    for step in (1, count - 1):
        peer = lax.rem(line + step, jnp.int32(count))
        pl.semaphore_signal(barrier, inc=1, device_id={"shard": peer}, device_id_type=MESH)


def await_plane_and_line():
    pl.semaphore_wait(pltpu.get_barrier_semaphore(), 5)


def line_copy(src, dst, sems, index, peer):
    return pltpu.make_async_remote_copy(
        src_ref=src,
        dst_ref=dst,
        send_sem=sems[0].at[index],
        recv_sem=sems[1].at[index],
        device_id={"shard": peer},
        device_id_type=MESH,
    )


KEY_PIECES = 4


def gather_keys_kernel(
    columns, w_ref, dy_ref, kv_ref, slots_ref, dy_all_ref, line_ref,
    send, recv, local, line_send, line_recv, line_local,
):
    me = lax.axis_index("rep")
    line = lax.axis_index("shard")
    count = line_ref.shape[0]
    start, width = columns
    piece = kv_ref.shape[0] // KEY_PIECES
    call_peers([flipped(me, k) for k in (1, 2, 4)])
    call_line(line, count)

    def place(k):
        return slots_ref.at[:, pl.ds(pl.multiple_of(k * width, width), width)]

    weights = Spread(
        me, w_ref.at[:, pl.ds(start, width)], place, (send.at[0], recv.at[0]), local.at[0]
    )
    blocks = Spread(
        me, dy_ref, lambda k: dy_all_ref.at[k], (send.at[1], recv.at[1]), local.at[1]
    )
    mine = pltpu.make_async_copy(kv_ref, line_ref.at[line], line_local)
    mine.start()

    def forward(step, part):
        rows = pl.ds(part * piece, piece)
        dst = line_ref.at[line - step, rows]
        src = kv_ref.at[rows] if step == 0 else dst
        sems = (line_send.at[step], line_recv.at[step])
        return line_copy(src, dst, sems, part, line + 1)

    def arrival(step, part):
        dst = line_ref.at[line - 1 - step, pl.ds(part * piece, piece)]
        return line_copy(dst, dst, (line_send.at[step], line_recv.at[step]), part, line - 1)

    def await_arrival(step, part):
        @pl.when(line >= step + 1)
        def _():
            arrival(step, part).wait_recv()

    def start_forward(step, part):
        @pl.when((line >= step) & (line < count - 1))
        def _():
            forward(step, part).start()

    await_plane_and_line()
    for part in range(KEY_PIECES):
        start_forward(0, part)
    weights.begin()
    blocks.begin()
    for step in range(1, count - 1):
        for part in range(KEY_PIECES):
            await_arrival(step - 1, part)
            start_forward(step, part)
        if step == 1:
            weights.middle()
        if step == 2:
            blocks.middle()
    weights.last()
    blocks.last()
    weights.end()
    blocks.end()
    for part in range(KEY_PIECES):
        await_arrival(count - 2, part)
    for step in range(count - 1):

        @pl.when((line >= step) & (line < count - 1))
        def _():
            for part in range(KEY_PIECES):
                forward(step, part).wait_send()

    mine.wait()


def gather_keys(weights, columns, block, kv_own, count, number):
    return pl.pallas_call(
        functools.partial(gather_keys_kernel, columns),
        in_specs=[pl.BlockSpec(memory_space=pl.ANY)] * 3,
        out_specs=[pl.BlockSpec(memory_space=pl.ANY)] * 3,
        out_shape=[
            jax.ShapeDtypeStruct((weights.shape[0], 8 * columns[1]), weights.dtype),
            jax.ShapeDtypeStruct((8, *block.shape), block.dtype),
            jax.ShapeDtypeStruct((count, *kv_own.shape), kv_own.dtype),
        ],
        scratch_shapes=[
            pltpu.SemaphoreType.DMA((2, 7)),
            pltpu.SemaphoreType.DMA((2, 7)),
            pltpu.SemaphoreType.DMA((2,)),
            pltpu.SemaphoreType.DMA((count - 1, KEY_PIECES)),
            pltpu.SemaphoreType.DMA((count - 1, KEY_PIECES)),
            pltpu.SemaphoreType.DMA,
        ],
        compiler_params=pltpu.CompilerParams(collective_id=number, has_side_effects=True),
        name="gather_keys",
    )(weights, block, kv_own)


def column_slice(ref, start, width):
    return ref[:, pl.ds(pl.multiple_of(start, width), width)]


def send_all(me, peers, bufs, places, sems, local):
    count = len(bufs)
    own = [
        pltpu.make_async_copy(bufs[i].at[0], places[i](0), local.at[i]) for i in range(count)
    ]
    moves = [
        [
            remote(bufs[i].at[k], places[i](k), (sems[0].at[i], sems[1].at[i]), k, peers[k - 1])
            for k in (7, 6, 5, 4, 3, 2, 1)
        ]
        for i in range(count)
    ]
    for i in range(count):
        own[i].start()
        for move in moves[i]:
            move.start()
    for i in range(count):
        for move in moves[i]:
            move.wait()
        own[i].wait()


def swap_first_kernel(proj_ref, out_w_ref, out_ref, buf, send, recv, local):
    me = lax.axis_index("rep")
    peers = [flipped(me, k) for k in range(1, 8)]
    call_peers(peers)
    q_all = QUERY_HEADS * HEAD_SIZE
    kv_all = KEY_VALUE_HEADS * HEAD_SIZE
    for k in range(8):
        to = peers[k - 1] if k else me
        odd = lax.rem(to, jnp.int32(2)) == 1
        pair = lax.div(to, jnp.int32(2)) * 128
        key = column_slice(proj_ref, q_all + pair, 128)
        value = column_slice(proj_ref, q_all + kv_all + pair, 128)
        lane = lax.broadcasted_iota(jnp.int32, key.shape, 1)
        key = jnp.where(odd, swap_halves(key), key)
        value = jnp.where(odd, value, swap_halves(value))
        buf[k, :, 0:256] = to_bf(column_slice(proj_ref, to * 256, 256))
        buf[k, :, 256:384] = to_bf(jnp.where(lane < HEAD_SIZE, key, value))
        buf[k, :, 384:640] = to_bf(column_slice(out_w_ref, to * 256, 256))
    await_peers(peers)
    send_all(me, peers, (buf,), (lambda k: out_ref.at[me],), (send, recv), local)


def swap_first(proj_w, out_w_t):
    owned = proj_w.shape[0]
    return pl.pallas_call(
        swap_first_kernel,
        in_specs=[pl.BlockSpec(memory_space=pltpu.VMEM)] * 2,
        out_specs=pl.BlockSpec(memory_space=pl.ANY),
        out_shape=jax.ShapeDtypeStruct((8, owned, 640), jnp.bfloat16),
        scratch_shapes=[
            pltpu.VMEM((8, owned, 640), jnp.bfloat16),
            pltpu.SemaphoreType.DMA((1, 8)),
            pltpu.SemaphoreType.DMA((1, 8)),
            pltpu.SemaphoreType.DMA((1,)),
        ],
        compiler_params=pltpu.CompilerParams(
            collective_id=7, has_side_effects=True, vmem_limit_bytes=VMEM_BYTES
        ),
        name="swap_first",
    )(proj_w, out_w_t)


def swap_ffn_kernel(gu_ref, down_ref, out_a, out_b, buf_a, buf_b, send, recv, local):
    me = lax.axis_index("rep")
    peers = [flipped(me, k) for k in range(1, 8)]
    call_peers(peers)
    for half, buf in enumerate((buf_a, buf_b)):
        for k in range(8):
            to = peers[k - 1] if k else me
            at = half * (FF // 2) + to * 512
            buf[k, :, 0:512] = to_bf(column_slice(gu_ref, at, 512))
            buf[k, :, 512:1024] = to_bf(column_slice(gu_ref, FF + at, 512))
            buf[k, :, 1024:1536] = to_bf(column_slice(down_ref, at, 512))
    await_peers(peers)
    send_all(
        me,
        peers,
        (buf_a, buf_b),
        (lambda k: out_a.at[me], lambda k: out_b.at[me]),
        (send, recv),
        local,
    )


def swap_ffn(gu_w, down_w_t):
    owned = gu_w.shape[0]
    wide = (8, owned, 1536)
    return pl.pallas_call(
        swap_ffn_kernel,
        in_specs=[pl.BlockSpec(memory_space=pltpu.VMEM)] * 2,
        out_specs=[pl.BlockSpec(memory_space=pl.ANY)] * 2,
        out_shape=[jax.ShapeDtypeStruct(wide, jnp.bfloat16)] * 2,
        scratch_shapes=[
            pltpu.VMEM(wide, jnp.bfloat16),
            pltpu.VMEM(wide, jnp.bfloat16),
            pltpu.SemaphoreType.DMA((2, 8)),
            pltpu.SemaphoreType.DMA((2, 8)),
            pltpu.SemaphoreType.DMA((2,)),
        ],
        compiler_params=pltpu.CompilerParams(
            collective_id=8, has_side_effects=True, vmem_limit_bytes=VMEM_BYTES
        ),
        name="swap_ffn",
    )(gu_w, down_w_t)


def swap_back_kernel(layout, *refs):
    outs = 1 + max(entry[3] for entry in layout)
    sources, results = refs, refs[-3 - outs : -3]
    send, recv, local = refs[-3:]
    me = lax.axis_index("rep")
    peers = [flipped(me, k) for k in range(1, 8)]
    call_peers(peers)
    own, moves = [], []
    for n, (i, start, width, o, at) in enumerate(layout):

        def piece(to):
            return sources[i].at[to, :, pl.ds(start, width)]

        place = results[o].at[:, pl.ds(pl.multiple_of(at + me * width, 128), width)]
        own.append(pltpu.make_async_copy(piece(me), place, local.at[n]))
        moves.append(
            [
                remote(piece(peers[k - 1]), place, (send.at[n], recv.at[n]), k, peers[k - 1])
                for k in (7, 6, 5, 4, 3, 2, 1)
            ]
        )
    for move in own:
        move.start()
    await_peers(peers)
    for group in moves:
        for move in group:
            move.start()
    for group, mine in zip(moves, own):
        for move in group:
            move.wait()
        mine.wait()


def swap_back(sources, layout, widths, number, earlier=()):
    aliases = {len(sources) + i: i for i in range(len(earlier))}
    sources = [source.reshape(8, -1, source.shape[1]) for source in sources]
    owned = sources[0].shape[1]
    return pl.pallas_call(
        functools.partial(swap_back_kernel, layout),
        in_specs=[pl.BlockSpec(memory_space=pl.ANY)] * (len(sources) + len(earlier)),
        out_specs=[pl.BlockSpec(memory_space=pl.ANY)] * len(widths),
        out_shape=[jax.ShapeDtypeStruct((owned, width), jnp.bfloat16) for width in widths],
        input_output_aliases=aliases,
        scratch_shapes=[
            pltpu.SemaphoreType.DMA((len(layout), 8)),
            pltpu.SemaphoreType.DMA((len(layout), 8)),
            pltpu.SemaphoreType.DMA((len(layout),)),
        ],
        compiler_params=pltpu.CompilerParams(collective_id=number, has_side_effects=True),
        name=f"swap_back_{number}",
    )(*sources, *earlier)


def ffn_first_kernel(
    x_ref, dy_ref, w_ref, xall_ref, hid_ref, dgu_ref,
    x_buf, dy_buf, w_buf, hid_buf, dgu_buf, send, recv, w_sem, dy_sem, x_sem, out_sem,
):
    me = lax.axis_index("rep")
    first, second, sibling, one, two = corner_route(me)
    peers = [flipped(me, k) for k in (1, 2, 4)]
    width = hid_ref.shape[2]
    sems = (send, recv)
    loads = [
        pltpu.make_async_copy(w_ref.at[:, pl.ds(i * width, width)], w_buf.at[i], w_sem.at[i])
        for i in range(3)
    ]

    def dy_load(k):
        return pltpu.make_async_copy(dy_ref.at[k], dy_buf.at[k], dy_sem.at[k])

    call_peers(peers)
    mine = pltpu.make_async_copy(x_ref, x_buf.at[0], x_sem.at[0])
    mine.start()
    dy_load(0).start()
    for copy in loads:
        copy.start()
    for k in range(1, 8):
        dy_load(k).start()
    to_sibling = remote(x_buf.at[0], x_buf.at[1], sems, 0, sibling)
    to_one = remote(x_buf.at[0], x_buf.at[first], sems, 1, one)
    to_two = remote(x_buf.at[0], x_buf.at[second], sems, 2, two)
    corner = remote(x_buf.at[second], x_buf.at[6], sems, 3, one)
    pass_first = remote(x_buf.at[first], x_buf.at[first + 1], sems, 4, sibling)
    pass_second = remote(x_buf.at[second], x_buf.at[second + 1], sems, 5, sibling)
    pass_corner = remote(x_buf.at[6], x_buf.at[7], sems, 6, sibling)
    mine.wait()
    await_peers(peers)
    to_one.start()
    to_two.start()
    to_sibling.start()
    for copy in loads:
        copy.wait()

    def results(k):
        return (
            pltpu.make_async_copy(hid_buf.at[k], hid_ref.at[k], out_sem.at[0, k]),
            pltpu.make_async_copy(dgu_buf.at[k], dgu_ref.at[k], out_sem.at[1, k]),
        )

    def work(k):
        dy_load(k).wait()

        @pl.loop(0, width // 256)
        def _(j):
            at = pl.multiple_of(j * 256, 256)
            cols = pl.ds(at, 256)
            x = x_buf[k]
            gate = dot(x, w_buf[0, :, cols])
            up = dot(x, w_buf[1, :, cols])
            grad_hidden = dot(dy_buf[k], w_buf[2, :, cols])
            sig = 1.0 / (1.0 + jnp.exp(-gate))
            silu = gate * sig
            hid_buf[k, :, cols] = to_bf(silu * up)
            dgu_buf[k, :, cols] = to_bf(grad_hidden * up * sig * (1.0 + gate * (1.0 - sig)))
            dgu_buf[k, :, pl.ds(width + at, 256)] = to_bf(grad_hidden * silu)

        for copy in results(k):
            copy.start()

    work(0)
    to_sibling.wait_recv()
    work(1)
    to_two.wait_recv()
    corner.start()
    pass_second.start()
    to_one.wait_recv()
    pass_first.start()
    work(first)
    work(second)
    pass_first.wait_recv()
    work(second + 1)
    corner.wait_recv()
    pass_corner.start()
    pass_second.wait_recv()
    work(first + 1)
    work(6)
    pass_corner.wait_recv()
    keep = pltpu.make_async_copy(x_buf, xall_ref, x_sem.at[1])
    keep.start()
    work(7)
    for copy in (to_sibling, to_one, to_two, corner, pass_first, pass_second, pass_corner):
        copy.wait_send()
    keep.wait()

    for k in range(8):
        for copy in results(k):
            copy.wait()


def ffn_first(x, dy_all, weights):
    _, rows, depth = dy_all.shape
    width = weights.shape[1] // 3
    shapes = [(8, rows, depth), (8, rows, width), (8, rows, 2 * width)]
    return pl.pallas_call(
        ffn_first_kernel,
        in_specs=[pl.BlockSpec(memory_space=pl.ANY)] * 3,
        out_specs=[pl.BlockSpec(memory_space=pl.ANY)] * 3,
        out_shape=[jax.ShapeDtypeStruct(shape, jnp.bfloat16) for shape in shapes],
        scratch_shapes=[
            pltpu.VMEM((8, rows, depth), jnp.bfloat16),
            pltpu.VMEM((8, rows, depth), jnp.bfloat16),
            pltpu.VMEM((3, depth, width), jnp.bfloat16),
            pltpu.VMEM((8, rows, width), jnp.bfloat16),
            pltpu.VMEM((8, rows, 2 * width), jnp.bfloat16),
            pltpu.SemaphoreType.DMA((7,)),
            pltpu.SemaphoreType.DMA((7,)),
            pltpu.SemaphoreType.DMA((3,)),
            pltpu.SemaphoreType.DMA((8,)),
            pltpu.SemaphoreType.DMA((2,)),
            pltpu.SemaphoreType.DMA((2, 8)),
        ],
        compiler_params=pltpu.CompilerParams(
            collective_id=3, has_side_effects=True, vmem_limit_bytes=VMEM_BYTES
        ),
        name="ffn_first",
    )(x, dy_all, weights)


def ffn_gradient_kernel(x_ref, dy_ref, dgu_ref, hid_ref, out_ref):
    rows = x_ref.shape[0] * x_ref.shape[1]
    x = x_ref[...].reshape(rows, -1)
    dy = dy_ref[...].reshape(rows, -1)
    both = dgu_ref.shape[2]
    for at in range(0, both, 512):
        part = dgu_ref[:, :, at : at + 512].reshape(rows, -1)
        out_ref[:, at : at + 512] = to_bf(outer_rows(x, part))
    out_ref[:, both:] = to_bf(outer_rows(dy, hid_ref[...].reshape(rows, -1)))


def ffn_gradient(x_all, dy_all, dgu, hid):
    slots, rows, depth = x_all.shape
    both, width = dgu.shape[2], hid.shape[2]
    return pl.pallas_call(
        ffn_gradient_kernel,
        grid=(depth // 256,),
        in_specs=[
            pl.BlockSpec((slots, rows, 256), lambda i: (0, 0, i)),
            pl.BlockSpec((slots, rows, 256), lambda i: (0, 0, i)),
            pl.BlockSpec((slots, rows, both), lambda i: (0, 0, 0)),
            pl.BlockSpec((slots, rows, width), lambda i: (0, 0, 0)),
        ],
        out_specs=pl.BlockSpec((256, both + width), lambda i: (i, 0)),
        out_shape=jax.ShapeDtypeStruct((depth, both + width), jnp.bfloat16),
        compiler_params=pltpu.CompilerParams(vmem_limit_bytes=VMEM_BYTES),
        name="ffn_gradient",
    )(x_all, dy_all, dgu, hid)


def ffn_second_kernel(
    x_ref, dy_ref, w_ref, hid_a_ref, dgu_a_ref, w_a_ref, hid_ref, dgu_ref, out_ref, layer_ref,
    x_buf, dy_buf, w_buf, wa_buf, hid_a_buf, dgu_a_buf, hid_buf, dgu_buf,
    to_buf, from_buf, layer_to, layer_from,
    send, recv, layer_send, layer_recv, w_sem, in_sem, out_sem,
):
    me = lax.axis_index("rep")
    peers = [flipped(me, k) for k in (1, 2, 4)]
    call_peers(peers)
    width = hid_ref.shape[2]
    loads = [
        pltpu.make_async_copy(w_ref.at[:, pl.ds(i * width, width)], w_buf.at[i], w_sem.at[i])
        for i in range(3)
    ]
    loads.append(pltpu.make_async_copy(w_a_ref, wa_buf, w_sem.at[3]))

    def block_loads(n, k):
        pairs = (
            (x_ref, x_buf), (dy_ref, dy_buf), (hid_a_ref, hid_a_buf), (dgu_a_ref, dgu_a_buf)
        )
        return [
            pltpu.make_async_copy(ref.at[k], buf.at[n % 2], in_sem.at[i, n % 2])
            for i, (ref, buf) in enumerate(pairs)
        ]

    def results(n, k):
        gate_at, up_at = pl.ds(0, width), pl.ds(width, width)
        pairs = (
            (hid_buf.at[n % 2], hid_ref.at[k]),
            (dgu_buf.at[0, n % 2], dgu_ref.at[k, :, gate_at]),
            (dgu_buf.at[1, n % 2], dgu_ref.at[k, :, up_at]),
        )
        return [
            pltpu.make_async_copy(src, dst, out_sem.at[i, n % 2])
            for i, (src, dst) in enumerate(pairs)
        ]

    def work(n):
        def tile(at):
            x = x_buf[n % 2]
            gate = dot(x, w_buf[0, :, at])
            up = dot(x, w_buf[1, :, at])
            grad_hidden = dot(dy_buf[n % 2], w_buf[2, :, at])
            sig = 1.0 / (1.0 + jnp.exp(-gate))
            silu = gate * sig
            hid_buf[n % 2, :, at] = to_bf(silu * up)
            dgu_buf[0, n % 2, :, at] = to_bf(grad_hidden * up * sig * (1.0 + gate * (1.0 - sig)))
            dgu_buf[1, n % 2, :, at] = to_bf(grad_hidden * silu)

        column_tiles(width // 256, tile)

    gate_up_at, down_at = pl.ds(0, 2 * width), pl.ds(2 * width, width)
    turn = [0]

    def product(k, write):
        n = turn[0]

        def tile(at):
            value = contract_last(dgu_a_buf[n % 2], wa_buf[at, gate_up_at])
            value = value + contract_last(dgu_buf[0, n % 2], w_buf[0, at, :])
            write(at, value + contract_last(dgu_buf[1, n % 2], w_buf[1, at, :]))

        column_tiles(out_ref.shape[1] // 256, tile)

    def layer_product(k, write):
        n = turn[0]

        def tile(at):
            value = contract_last(hid_a_buf[n % 2], wa_buf[at, down_at])
            write(at, value + contract_last(hid_buf[n % 2], w_buf[2, at, :]))

        column_tiles(out_ref.shape[1] // 256, tile)

    total = PlaneSum(me, product, out_ref, to_buf, from_buf, (send, recv))
    layer = PlaneSum(me, layer_product, layer_ref, layer_to, layer_from, (layer_send, layer_recv))
    for copy in (*block_loads(0, total.order[0]), *loads):
        copy.start()
    for copy in loads:
        copy.wait()
    await_peers(peers)
    for n, k in enumerate(total.order):
        turn[0] = n
        if n < 7:
            for copy in block_loads(n + 1, total.order[n + 1]):
                copy.start()
        for copy in block_loads(n, k):
            copy.wait()
        if n > 1:
            for copy in results(n - 2, total.order[n - 2]):
                copy.wait()
        work(n)
        for copy in results(n, k):
            copy.start()
        total.stage(n)
        layer.stage(n)
    total.end()
    layer.end()
    for n in (6, 7):
        for copy in results(n, total.order[n]):
            copy.wait()


def ffn_second(x, dy_all, weights, hid_a, dgu_a, weights_a):
    _, rows, depth = x.shape
    width = weights.shape[1] // 3
    bf = jnp.bfloat16
    return pl.pallas_call(
        ffn_second_kernel,
        in_specs=[pl.BlockSpec(memory_space=pl.ANY)] * 6,
        out_specs=[pl.BlockSpec(memory_space=pl.ANY)] * 2
        + [pl.BlockSpec(memory_space=pltpu.VMEM)] * 2,
        out_shape=[
            jax.ShapeDtypeStruct((8, rows, width), bf),
            jax.ShapeDtypeStruct((8, rows, 2 * width), bf),
            jax.ShapeDtypeStruct((rows, depth), jnp.float32),
            jax.ShapeDtypeStruct((rows, depth), jnp.float32),
        ],
        scratch_shapes=[
            pltpu.VMEM((2, rows, depth), bf),
            pltpu.VMEM((2, rows, depth), bf),
            pltpu.VMEM((3, depth, width), bf),
            pltpu.VMEM((depth, 3 * width), bf),
            pltpu.VMEM((2, rows, width), bf),
            pltpu.VMEM((2, rows, 2 * width), bf),
            pltpu.VMEM((2, rows, width), bf),
            pltpu.VMEM((2, 2, rows, width), bf),
            pltpu.VMEM((7, rows, depth), bf),
            pltpu.VMEM((7, rows, depth), bf),
            pltpu.VMEM((7, rows, depth), bf),
            pltpu.VMEM((7, rows, depth), bf),
            pltpu.SemaphoreType.DMA((7,)),
            pltpu.SemaphoreType.DMA((7,)),
            pltpu.SemaphoreType.DMA((7,)),
            pltpu.SemaphoreType.DMA((7,)),
            pltpu.SemaphoreType.DMA((4,)),
            pltpu.SemaphoreType.DMA((4, 2)),
            pltpu.SemaphoreType.DMA((3, 2)),
        ],
        compiler_params=pltpu.CompilerParams(
            collective_id=4, has_side_effects=True, vmem_limit_bytes=VMEM_BYTES
        ),
        name="ffn_second",
    )(x, dy_all, weights, hid_a, dgu_a, weights_a)


class PlaneSum:
    def __init__(self, me, product, out_ref, to_buf, from_buf, sems):
        self.first, self.second, sibling, one, two = corner_route(me)
        self.product, self.out_ref = product, out_ref
        self.to_buf, self.from_buf = to_buf, from_buf

        def copy(i, peer):
            return lambda: remote(to_buf.at[i], from_buf.at[i], sems, i, peer)

        self.given = [copy(i, sibling) for i in range(4)]
        self.corner, self.to_one, self.to_two = copy(4, one), copy(5, one), copy(6, two)
        self.order = (7, 6, self.second + 1, self.first, self.first + 1, self.second, 1, 0)

    def give(self, k, i):
        def write(at, value):
            self.to_buf[i, :, at] = to_bf(value)

        self.product(k, write)
        self.given[i]().start()

    def pass_on(self, k, i, o, move, extra=None):
        def write(at, value):
            value = value + to_f32(self.from_buf[i, :, at])
            if extra is not None:
                value = value + to_f32(self.from_buf[extra, :, at])
            self.to_buf[o, :, at] = to_bf(value)

        self.given[i]().wait_recv()
        self.product(k, write)
        move().start()

    def stage(self, number):
        if number == 0:
            self.give(7, 0)
        elif number == 1:
            self.pass_on(6, 0, 4, self.corner)
        elif number == 2:
            self.give(self.second + 1, 1)
        elif number == 3:
            self.pass_on(self.first, 1, 5, self.to_one)
        elif number == 4:
            self.give(self.first + 1, 2)
        elif number == 5:
            self.corner().wait_recv()
            self.pass_on(self.second, 2, 6, self.to_two, 4)
        elif number == 6:
            self.give(1, 3)
        else:

            def keep(at, value):
                self.out_ref[:, at] = value

            self.product(0, keep)

    def end(self):
        self.given[3]().wait_recv()
        self.to_one().wait_recv()
        self.to_two().wait_recv()

        @pl.loop(0, self.out_ref.shape[1] // 256)
        def _(j):
            at = pl.ds(pl.multiple_of(j * 256, 256), 256)
            self.out_ref[:, at] += (
                to_f32(self.from_buf[3, :, at])
                + to_f32(self.from_buf[5, :, at])
                + to_f32(self.from_buf[6, :, at])
            )

        for move in (*self.given, self.corner, self.to_one, self.to_two):
            move().wait_send()


def column_tiles(count, body):
    @pl.loop(0, count)
    def _(j):
        body(pl.ds(pl.multiple_of(j * 256, 256), 256))


def product_sum_kernel(offsets, depths, *refs):
    count = len(depths)
    lefts, rights = refs[:count], refs[count : 2 * count]
    out_ref, left_buf, right_buf, to_buf, from_buf, send, recv, load_sem, left_sem = refs[
        2 * count :
    ]
    me = lax.axis_index("rep")
    peers = [flipped(me, k) for k in (1, 2, 4)]
    starts = [sum(depths[:i]) for i in range(len(depths))]
    call_peers(peers)
    right_loads = [
        pltpu.make_async_copy(
            rights[i].at[:, pl.ds(offsets[i], depths[i])],
            right_buf.at[:, pl.ds(starts[i], depths[i])],
            load_sem.at[i],
        )
        for i in range(count)
    ]
    for copy in right_loads:
        copy.start()

    def load(k, i):
        return pltpu.make_async_copy(
            lefts[i].at[k], left_buf.at[k, :, pl.ds(starts[i], depths[i])], left_sem.at[k, i]
        )

    def product(k, write):
        for i in range(count):
            load(k, i).wait()
        column_tiles(
            right_buf.shape[0] // 256,
            lambda at: write(at, contract_last(left_buf[k], right_buf[at, :])),
        )

    total = PlaneSum(me, product, out_ref, to_buf, from_buf, (send, recv))
    for k in total.order:
        for i in range(count):
            load(k, i).start()
    await_peers(peers)
    for copy in right_loads:
        copy.wait()
    for number in range(8):
        total.stage(number)
    total.end()


def product_sum(lefts, rights, offsets, number):
    depths = [left.shape[2] for left in lefts]
    rows = lefts[0].shape[1]
    wide = rights[0].shape[0]
    return pl.pallas_call(
        functools.partial(product_sum_kernel, offsets, depths),
        in_specs=[pl.BlockSpec(memory_space=pl.ANY)] * (2 * len(lefts)),
        out_specs=pl.BlockSpec(memory_space=pltpu.VMEM),
        out_shape=jax.ShapeDtypeStruct((rows, wide), jnp.float32),
        scratch_shapes=[
            pltpu.VMEM((8, rows, sum(depths)), jnp.bfloat16),
            pltpu.VMEM((wide, sum(depths)), jnp.bfloat16),
            pltpu.VMEM((7, rows, wide), jnp.bfloat16),
            pltpu.VMEM((7, rows, wide), jnp.bfloat16),
            pltpu.SemaphoreType.DMA((7,)),
            pltpu.SemaphoreType.DMA((7,)),
            pltpu.SemaphoreType.DMA((len(lefts),)),
            pltpu.SemaphoreType.DMA((8, len(lefts))),
        ],
        compiler_params=pltpu.CompilerParams(
            collective_id=number, has_side_effects=True, vmem_limit_bytes=VMEM_BYTES
        ),
        name=f"product_sum_{number}",
    )(*lefts, *rights)


def on_plane_of_8(
    tokens,
    cotangent,
    segment_ids,
    positions,
    projection_weight,
    projection_first_moment,
    projection_second_moment,
    out_weight,
    out_first,
    out_second,
    gate_up_weight,
    gate_up_first,
    gate_up_second,
    down_weight,
    down_first,
    down_second,
    norm_gains,
    gains_first,
    gains_second,
):
    shard_count = lax.axis_size("shard")
    shard_pos = lax.axis_index("shard")
    me = lax.axis_index("rep")
    token_rows = tokens.shape[0]
    group_rows = segment_ids.shape[0]
    plane_rows = 8 * token_rows
    owned = norm_gains.shape[1]
    q_width = QUERY_HEADS * HEAD_SIZE // 8

    def flat(parts):
        return parts.reshape(plane_rows, -1)

    def line_gather(parts):
        return lax.all_gather(flat_rows(parts), "shard", axis=0, tiled=True)

    def flat_rows(parts):
        return parts.reshape(8 * owned, -1)

    def line_sum(grad):
        return lax.psum_scatter(to_bf(grad), "shard", scatter_dimension=0, tiled=True)

    gains_b = to_f32(to_bf(norm_gains))
    turns = [gains_b] + [
        lax.ppermute(gains_b, "shard", [(i, (i - d) % shard_count) for i in range(shard_count)])
        for d in range(1, shard_count)
    ]
    gains_line = jnp.take(
        jnp.stack(turns), (jnp.arange(shard_count) - shard_pos) % shard_count, axis=0
    )
    gains_size = shard_count * 2 * owned
    notes = jnp.concatenate([gains_line.reshape(-1), to_f32(segment_ids)])
    cos_own, sin_own = tables(positions)
    angles = HEAD_SIZE // 2
    table_own = jnp.concatenate([cos_own[:, :angles], sin_own[:, :angles]], axis=1)
    table_own = jnp.pad(table_own, ((0, 0), (0, 128 - 2 * angles)))
    notes = jnp.pad(notes, (0, -notes.shape[0] % 1024)).reshape(8, -1)

    first_parts = swap_first(projection_weight, out_weight.T)
    first_w = line_gather(first_parts)
    ffn_parts = swap_ffn(after(gate_up_weight, first_parts), down_weight.T)
    ffn_a = line_gather(ffn_parts[0])
    tokens_all, notes_all, table = plane_gather(
        [after(tokens, ffn_parts[0]), notes, table_own], (None,) * 3, 9
    )
    notes_all = notes_all.reshape(8, -1)
    gain_full = (
        jnp.take(notes_all[:, :gains_size], jnp.arange(8) ^ me, axis=0)
        .reshape(8, shard_count, 2, owned)
        .transpose(2, 1, 0, 3)
        .reshape(2, MODEL_WIDTH)
    )
    gain_one = gain_full[0]
    gain_two = gain_full[1]
    seg_k = notes_all[:, gains_size : gains_size + group_rows]
    seg_q = lax.dynamic_slice_in_dim(seg_k, shard_pos * token_rows, token_rows, 1)

    normed_one, query_b, kv_own = project(tokens_all, first_w, gain_one[None, :], table)
    normed_one = flat(normed_one)
    ffn_b = line_gather(after(ffn_parts[1], tokens_all))
    out_slots, cotangent_all, kv_line = gather_keys(
        first_w, (q_width + 2 * HEAD_SIZE, q_width), cotangent, kv_own, shard_count, 10
    )
    seg_q_column, seg_k_row = seg_q[:, :, None], seg_k[:, None, :]
    seg_q_row, seg_k_column = seg_q[:, None, :], seg_k[:, :, None]
    out_b, logs, out_own = attend(query_b, kv_line, seg_q_column, seg_k_row)
    tokens_f = to_f32(tokens)
    hidden_one = tokens_f + contract_last(out_own, out_slots)
    scale_two = rms_scale(hidden_one)
    normed_two_own = to_bf(hidden_one * scale_two * gain_two)
    normed_two, hid_a, dgu_a = ffn_first(normed_two_own, cotangent_all, ffn_a)
    grad_a = ffn_gradient(normed_two, cotangent_all, dgu_a, hid_a)
    sum_a = line_sum(grad_a)
    x_late, seg_k_column, log_rows, _ = lax.optimization_barrier(
        (normed_two, seg_k_column, logs.transpose(0, 2, 1), grad_a)
    )
    hid_b, dgu_b, grad_normed_two, layer_sum = ffn_second(
        x_late, cotangent_all, ffn_b, hid_a, dgu_a, ffn_a
    )
    grad_hidden_one = to_f32(cotangent) + norm_back(
        hidden_one, scale_two, gain_two, grad_normed_two
    )
    grad_attn = to_bf(grad_hidden_one)
    grad_b = ffn_gradient(normed_two, cotangent_all, dgu_b, hid_b)
    sum_b = line_sum(grad_b)
    grad_q, grad_kv_line, grad_attn_all = attend_back(
        after(to_bf(dot(grad_attn, out_slots)), sum_a, grad_b),
        grad_attn,
        query_b,
        kv_line,
        seg_q_row,
        seg_k_column,
        log_rows,
        table,
    )
    layer_out = to_bf(hidden_one + layer_sum)
    grad_out = to_bf(outer_rows(flat(grad_attn_all), out_b))
    grad_first = jnp.concatenate([to_bf(outer_rows(normed_one, grad_q)), grad_out], axis=1)
    half = FF // 2

    def ffn_layout(at):
        return ((0, 0, 512, 0, at), (0, 512, 512, 0, FF + at), (0, 1024, 512, 1, at))

    sizes = (2 * FF, FF)
    grads_a = swap_back([after(sum_a, grad_first)], ffn_layout(0), sizes, 13)
    grad_kv = lax.psum_scatter(
        after(grad_kv_line, sum_b, *grads_a), "shard", scatter_dimension=0
    )
    grad_gu_w, grad_down_w = swap_back([sum_b], ffn_layout(half), sizes, 15, grads_a)
    grad_kv = after(grad_kv, grad_gu_w)
    sum_first = line_sum(after(grad_first, grad_kv))
    grad_gu_w = to_f32(grad_gu_w)
    grad_down_w = to_f32(grad_down_w).T
    new_gu = adamw(gate_up_weight, gate_up_first, gate_up_second, grad_gu_w, RATES[2], DECAYS[2])
    new_down = adamw(down_weight, down_first, down_second, grad_down_w, RATES[3], DECAYS[3])
    grad_kv = to_f32(grad_kv)
    angle_rows = flat(table)
    cos_table = jnp.concatenate([angle_rows[:, :angles]] * 2, axis=1)
    sin_table = jnp.concatenate([angle_rows[:, angles : 2 * angles]] * 2, axis=1)
    grad_kv_b = to_bf(
        jnp.concatenate(
            [rotate(grad_kv[:, :HEAD_SIZE], cos_table, sin_table, -1.0), grad_kv[:, HEAD_SIZE:]],
            axis=1,
        )
    )
    grad_kv_proj = to_bf(outer_rows(normed_one, grad_kv_b))
    sum_kv = line_sum(grad_kv_proj)
    grad_normed_one = product_sum(
        [
            after(grad_q, grad_kv_proj).reshape(8, token_rows, -1),
            grad_kv_b.reshape(8, token_rows, -1),
        ],
        [first_w, first_w],
        (0, q_width),
        6,
    )
    back_one = norm_back(tokens_f, rms_scale(tokens_f), gain_one, grad_normed_one)
    tokens_grad = to_bf(grad_hidden_one + back_one)

    grad_q_w, grad_kv_w, grad_out_w = swap_back(
        [sum_first, sum_kv],
        ((0, 0, 256, 0, 0), (1, 0, 128, 1, 0), (0, 256, 256, 2, 0)),
        (8 * q_width, 8 * 128, 8 * q_width),
        14,
    )
    grad_kv_w = grad_kv_w.reshape(owned, 8, 2, HEAD_SIZE).transpose(0, 2, 1, 3)
    grad_qkv_w = to_f32(jnp.concatenate([grad_q_w, grad_kv_w.reshape(owned, -1)], axis=1))
    grad_out_w = to_f32(grad_out_w).T
    grad_gain_w = (
        jnp.stack(
            [
                jnp.sum(to_f32(to_bf(projection_weight)) * grad_qkv_w, axis=1),
                jnp.sum(to_f32(to_bf(gate_up_weight)) * grad_gu_w, axis=1),
            ]
        )
        / gains_b
    )
    new_qkv = adamw(
        projection_weight,
        projection_first_moment,
        projection_second_moment,
        grad_qkv_w,
        RATES[0],
        DECAYS[0],
    )
    new_out = adamw(out_weight, out_first, out_second, grad_out_w, RATES[1], DECAYS[1])
    new_gain = adamw(norm_gains, gains_first, gains_second, grad_gain_w, RATES[4], DECAYS[4])
    return (layer_out, tokens_grad, *new_qkv, *new_out, *new_gu, *new_down, *new_gain)


def any_gather(block):
    return lax.all_gather(block, "rep", axis=0, tiled=True)


def any_sum(blocks):
    return to_f32(lax.psum_scatter(to_bf(blocks), "rep", scatter_dimension=0, tiled=True))


def any_swap(blocks):
    return lax.all_to_all(blocks, "rep", 0, 0, tiled=True)


def on_any_mesh(
    tokens,
    cotangent,
    segment_ids,
    positions,
    projection_weight,
    projection_first_moment,
    projection_second_moment,
    out_weight,
    out_first,
    out_second,
    gate_up_weight,
    gate_up_first,
    gate_up_second,
    down_weight,
    down_first,
    down_second,
    norm_gains,
    gains_first,
    gains_second,
):
    shard_count = lax.axis_size("shard")
    rep_count = lax.axis_size("rep")
    shard_pos = lax.axis_index("shard")
    token_rows = tokens.shape[0]
    group_rows = segment_ids.shape[0]
    plane_rows = rep_count * token_rows
    owned = norm_gains.shape[1]
    q_all = QUERY_HEADS * HEAD_SIZE
    kv_all = KEY_VALUE_HEADS * HEAD_SIZE
    sharers = max(1, rep_count // KEY_VALUE_HEADS)
    kv_heads = max(1, KEY_VALUE_HEADS // rep_count)
    q_heads = QUERY_HEADS // rep_count
    q_each = q_heads // kv_heads
    q_width = q_heads * HEAD_SIZE
    kv_width = kv_heads * HEAD_SIZE
    ff_width = FF // rep_count
    score_scale = HEAD_SIZE ** (-0.5)

    def pieces(rows, width):
        return to_bf(rows).reshape(owned, -1, width).transpose(1, 0, 2)

    def kv_pieces(rows):
        return jnp.repeat(pieces(rows, kv_width), sharers, axis=0)

    def whole(parts):
        mine = any_swap(parts).reshape(rep_count * owned, -1)
        return lax.all_gather(mine, "shard", axis=0, tiled=True)

    proj = whole(
        jnp.concatenate(
            [
                pieces(projection_weight[:, :q_all], q_width),
                kv_pieces(projection_weight[:, q_all : q_all + kv_all]),
                kv_pieces(projection_weight[:, q_all + kv_all :]),
            ],
            axis=2,
        )
    )
    out_w = whole(pieces(out_weight.T, q_width))
    gate_w = whole(pieces(gate_up_weight[:, :FF], ff_width))
    up_w = whole(pieces(gate_up_weight[:, FF:], ff_width))
    down_w = whole(pieces(down_weight.T, ff_width))

    gains_b = to_f32(to_bf(norm_gains))
    gains_line = lax.all_gather(gains_b, "shard", axis=0)
    notes = jnp.concatenate(
        [gains_line.reshape(-1), to_f32(positions), to_f32(segment_ids)]
    ).reshape(1, -1)
    notes_all = any_gather(notes)
    gains_size = shard_count * 2 * owned
    gain_full = (
        notes_all[:, :gains_size]
        .reshape(rep_count, shard_count, 2, owned)
        .transpose(2, 1, 0, 3)
        .reshape(2, MODEL_WIDTH)
    )
    gain_one = gain_full[0]
    gain_two = gain_full[1]
    plane_pos = notes_all[:, gains_size : gains_size + token_rows].reshape(plane_rows)
    plane_seg = notes_all[:, gains_size + token_rows :]

    tokens_all = to_f32(any_gather(tokens))
    normed_one = to_bf(tokens_all * rms_scale(tokens_all) * gain_one)
    qkv = dot(normed_one, proj)
    cos_table, sin_table = tables(plane_pos)
    query_b = to_bf(rotate(qkv[:, :q_width], cos_table, sin_table, 1.0))
    key_b = to_bf(rotate(qkv[:, q_width : q_width + kv_width], cos_table, sin_table, 1.0))
    value_b = to_bf(qkv[:, q_width + kv_width :])
    kv_line = lax.all_gather(jnp.concatenate([key_b, value_b], axis=1), "shard", axis=0)
    kv_groups = (
        kv_line.reshape(shard_count, rep_count, token_rows, 2 * kv_width)
        .transpose(1, 0, 2, 3)
        .reshape(rep_count, group_rows, 2, kv_heads, HEAD_SIZE)
    )
    key_groups = kv_groups[:, :, 0].transpose(0, 2, 1, 3)
    value_groups = kv_groups[:, :, 1].transpose(0, 2, 1, 3)

    def to_heads(flat):
        return flat.reshape(rep_count, token_rows, kv_heads, q_each, HEAD_SIZE).transpose(
            0, 2, 3, 1, 4
        )

    def from_heads(heads):
        return heads.transpose(0, 3, 1, 2, 4).reshape(plane_rows, q_width)

    query_heads = to_heads(query_b)
    row_at = shard_pos * token_rows + jnp.arange(token_rows, dtype=jnp.int32)
    causal = jnp.arange(group_rows, dtype=jnp.int32)[None, :] <= row_at[:, None]

    def masked_scores(q_one, k_one, seg_one):
        seg_rows = lax.dynamic_slice_in_dim(seg_one, shard_pos * token_rows, token_rows, 0)
        allowed = (seg_rows[:, None] == seg_one[None, :]) & causal
        scores = (
            jnp.einsum("hgqd,hkd->hgqk", q_one, k_one, preferred_element_type=jnp.float32)
            * score_scale
        )
        return jnp.where(allowed[None, None], scores, -1e30)

    def group_forward(packed):
        q_one, k_one, v_one, seg_one = packed
        scores = masked_scores(q_one, k_one, seg_one)
        peak_score = jnp.max(scores, axis=-1, keepdims=True)
        exp_total = jnp.sum(jnp.exp(scores - peak_score), axis=-1, keepdims=True)
        log_sum = peak_score + jnp.log(exp_total)
        probs = to_bf(jnp.exp(scores - log_sum))
        attended = jnp.einsum("hgqk,hkd->hgqd", probs, v_one, preferred_element_type=jnp.float32)
        return (to_bf(attended), log_sum)

    attended, log_sums = lax.map(
        group_forward, (query_heads, key_groups, value_groups, plane_seg)
    )
    out_b = from_heads(attended)
    tokens_f = to_f32(tokens)
    hidden_one = tokens_f + any_sum(contract_last(out_b, out_w))
    scale_two = rms_scale(hidden_one)
    normed_two = any_gather(to_bf(hidden_one * scale_two * gain_two))
    gate_part = dot(normed_two, gate_w)
    up_part = dot(normed_two, up_w)
    sigmoid_gate = jax.nn.sigmoid(gate_part)
    silu_gate = gate_part * sigmoid_gate
    hidden_b = to_bf(silu_gate * up_part)
    layer_out = to_bf(hidden_one + any_sum(contract_last(hidden_b, down_w)))

    cotangent_all = any_gather(cotangent)
    grad_hidden = dot(cotangent_all, down_w)
    grad_gate_b = to_bf(
        grad_hidden * up_part * sigmoid_gate * (1.0 + gate_part * (1.0 - sigmoid_gate))
    )
    grad_up_b = to_bf(grad_hidden * silu_gate)
    grad_normed_two = any_sum(
        contract_last(grad_gate_b, gate_w) + contract_last(grad_up_b, up_w)
    )
    grad_hidden_one = to_f32(cotangent) + norm_back(
        hidden_one, scale_two, gain_two, grad_normed_two
    )
    grad_attn_b = any_gather(to_bf(grad_hidden_one))
    out_grad_heads = to_heads(to_bf(dot(grad_attn_b, out_w)))

    def group_backward(packed):
        q_one, k_one, v_one, seg_one, d_one, log_sum = packed
        probs = jnp.exp(masked_scores(q_one, k_one, seg_one) - log_sum)
        grad_probs = jnp.einsum("hgqd,hkd->hgqk", d_one, v_one, preferred_element_type=jnp.float32)
        inner = jnp.sum(grad_probs * probs, axis=-1, keepdims=True)
        grad_scores = to_bf(probs * (grad_probs - inner))
        grad_q = (
            jnp.einsum("hgqk,hkd->hgqd", grad_scores, k_one, preferred_element_type=jnp.float32)
            * score_scale
        )
        grad_k = (
            jnp.einsum("hgqk,hgqd->khd", grad_scores, q_one, preferred_element_type=jnp.float32)
            * score_scale
        )
        grad_v = jnp.einsum(
            "hgqk,hgqd->khd", to_bf(probs), d_one, preferred_element_type=jnp.float32
        )
        both = jnp.stack([grad_k, grad_v], axis=1).reshape(group_rows, 2 * kv_width)
        return (grad_q, to_bf(both))

    grad_q, grad_kv = lax.map(
        group_backward,
        (query_heads, key_groups, value_groups, plane_seg, out_grad_heads, log_sums),
    )
    grad_kv = (
        grad_kv.reshape(rep_count, shard_count, token_rows, 2 * kv_width)
        .transpose(1, 0, 2, 3)
        .reshape(shard_count * plane_rows, 2 * kv_width)
    )
    grad_kv = to_f32(lax.psum_scatter(grad_kv, "shard", scatter_dimension=0, tiled=True))
    grad_qkv_b = to_bf(
        jnp.concatenate(
            [
                rotate(from_heads(grad_q), cos_table, sin_table, -1.0),
                rotate(grad_kv[:, :kv_width], cos_table, sin_table, -1.0),
                grad_kv[:, kv_width:],
            ],
            axis=1,
        )
    )
    grad_normed_one = any_sum(contract_last(grad_qkv_b, proj))
    back_one = norm_back(tokens_f, rms_scale(tokens_f), gain_one, grad_normed_one)
    tokens_grad = to_bf(grad_hidden_one + back_one)

    def owner_pieces(grad):
        summed = lax.psum_scatter(to_bf(grad), "shard", scatter_dimension=0, tiled=True)
        return to_f32(any_swap(summed.reshape(rep_count, owned, -1)))

    def row_of(parts):
        return parts.transpose(1, 0, 2).reshape(owned, -1)

    def kv_row_of(parts):
        return row_of(parts.reshape(-1, sharers, owned, kv_width).sum(axis=1))

    down_parts = owner_pieces(outer_rows(cotangent_all, hidden_b))
    gate_parts = owner_pieces(outer_rows(normed_two, grad_gate_b))
    up_parts = owner_pieces(outer_rows(normed_two, grad_up_b))
    out_parts = owner_pieces(outer_rows(grad_attn_b, out_b))
    proj_parts = owner_pieces(outer_rows(normed_one, grad_qkv_b))
    grad_down_w = row_of(down_parts).T
    grad_gu_w = jnp.concatenate([row_of(gate_parts), row_of(up_parts)], axis=1)
    grad_out_w = row_of(out_parts).T
    grad_qkv_w = jnp.concatenate(
        [
            row_of(proj_parts[..., :q_width]),
            kv_row_of(proj_parts[..., q_width : q_width + kv_width]),
            kv_row_of(proj_parts[..., q_width + kv_width :]),
        ],
        axis=1,
    )
    grad_gain_w = (
        jnp.stack(
            [
                jnp.sum(to_f32(to_bf(projection_weight)) * grad_qkv_w, axis=1),
                jnp.sum(to_f32(to_bf(gate_up_weight)) * grad_gu_w, axis=1),
            ]
        )
        / gains_b
    )
    new_qkv = adamw(
        projection_weight,
        projection_first_moment,
        projection_second_moment,
        grad_qkv_w,
        RATES[0],
        DECAYS[0],
    )
    new_out = adamw(out_weight, out_first, out_second, grad_out_w, RATES[1], DECAYS[1])
    new_gu = adamw(gate_up_weight, gate_up_first, gate_up_second, grad_gu_w, RATES[2], DECAYS[2])
    new_down = adamw(down_weight, down_first, down_second, grad_down_w, RATES[3], DECAYS[3])
    new_gain = adamw(norm_gains, gains_first, gains_second, grad_gain_w, RATES[4], DECAYS[4])
    return (layer_out, tokens_grad, *new_qkv, *new_out, *new_gu, *new_down, *new_gain)


def solution(mesh):
    rows = P(("rep", "shard"), None)
    wide = P(("shard", "rep"), None)
    tall = P(None, ("shard", "rep"))
    in_specs = (
        (rows, rows, P("rep"), P(("rep", "shard")))
        + (wide,) * 3
        + (tall,) * 3
        + (wide,) * 3
        + (tall,) * 6
    )
    out_specs = (rows, rows) + (wide,) * 3 + (tall,) * 3 + (wide,) * 3 + (tall,) * 6
    on_device = on_plane_of_8 if mesh.shape["rep"] == 8 else on_any_mesh
    return jax.shard_map(
        on_device, mesh=mesh, in_specs=in_specs, out_specs=out_specs, check_vma=False
    )
```

time: 4980 us -> 705 us (0.14)
  waiting for transfers between devices: 4420 us -> 35.3 us
  Pallas kernels: 0 us -> 556 us
  matrix products: 320 us -> 28.3 us
  other arithmetic: 153 us -> 41.7 us
    all_gather x10 -> x3, waiting for transfers between devices: 2150 us -> 16 us  [line_gather(): return lax.all_gather(flat_rows(parts), 'shard', axis=0, tiled=True)]
    unnamed x17 -> x8, waiting for transfers between devices: 2080 us -> 0.13 us
    pallas_call x0 -> x15, Pallas kernels: none -> 556 us  [the longest x1 92.7 us: ffn_second(): pl.pallas_call(ffn_second_kernel, in_specs=[pl.BlockSpec(memory_space=pl....]
    dot_general x60 -> x1, matrix products: 185 us -> 6.7 us  [dot(): return jnp.dot(left, right, preferred_element_type=jnp.float32)]
    reduce_scatter x3 -> x5, waiting for transfers between devices: 189 us -> 16.6 us  [the longest x1 11.1 us: on_plane_of_8(): lax.psum_scatter(after(grad_kv_line, sum_b, *grads_a), 'shard', scatter_d...]
    concatenate x1 -> x5, other arithmetic: 79.3 us -> 3.7 us  [the longest x1 1.51 us: on_plane_of_8(): jnp.concatenate([to_bf(outer_rows(normed_one, grad_q)), grad_out], axis=1)]
    dot_general x4 -> x1, matrix products: 76.4 us -> 6.21 us  [contract_last(): lax.dot_general(left, right, (((1,), (1,)), ((), ())), preferred_element_...]
  transfers between devices with their start and end apart: 15 -> 11, of which waited for: 14 -> 5; matrix products, arithmetic and copies ran while one was open for 5% -> 11% of each run, Pallas kernels for 0% -> 76%
where the time goes in v1:
time: 705 us; the launch traced here: 701 us
  Pallas kernels  556 us (79%)
  other arithmetic  41.7 us (6%)
  waiting for transfers between devices  35.3 us (5%)
  matrix products  28.3 us (4%)
  local copies, waits for them, and re-layouts  19.7 us (3%)
  between operations  14.9 us (2%)
    pallas_call x1, Pallas kernels, ffn_second(): pl.pallas_call(ffn_second_kernel, in_specs=[pl.BlockSpec(memory_space=pl....  92.7 us
    pallas_call x1, Pallas kernels, gather_keys(): pl.pallas_call(functools.partial(gather_keys_kernel, columns), in_specs=[...  81 us
    pallas_call x1, Pallas kernels, attend_back(): pl.pallas_call(attend_back_kernel, grid=(8,), in_specs=[pl.BlockSpec(memo...  57.9 us
    pallas_call x3, Pallas kernels, swap_back(): pl.pallas_call(functools.partial(swap_back_kernel, layout), in_specs=[pl....  54.5 us
    pallas_call x1, Pallas kernels, ffn_first(): pl.pallas_call(ffn_first_kernel, in_specs=[pl.BlockSpec(memory_space=pl.A...  51.2 us
    pallas_call x1, Pallas kernels, product_sum(): pl.pallas_call(functools.partial(product_sum_kernel, offsets, depths), in...  47.2 us
    pallas_call x1, Pallas kernels, plane_gather(): pl.pallas_call(functools.partial(gather_kernel, columns), in_specs=[pl.Bl...  43.2 us
    pallas_call x1, Pallas kernels, swap_ffn(): pl.pallas_call(swap_ffn_kernel, in_specs=[pl.BlockSpec(memory_space=pltpu...  41 us
  transfers between devices with their start and end apart: 11, of which 5 were waited for; matrix products, arithmetic and copies ran while one was open for 11% of the time, Pallas kernels for 76%

profile of v1, /device:TPU:0, one launch (start us, length us, event | category | flops | bytes accessed | tf_op | source)
XLA Modules:
  0.0 701.0 jit_solution(9345911740249401684)
XLA Ops:
  7.2 14.1 %swap_first.1 = bf16[8,64,640]{2,1,0:T(8,128)(2,1)} custom-call(f32[64,3072]{1,0:T(8,128)} %proj_ref.1, f32[64,2048]{1,0:T(8,128)} %bitcast.81), custom_call_target="tpu_custom_call" | custom-call | tf_op jit(solution)/shard_map/swap_first/pallas_call | solution.py:690
  21.4 41.0 %swap_ffn.1 = (bf16[8,64,1536]{2,1,0:T(8,128)(2,1)}, bf16[8,64,1536]{2,1,0:T(8,128)(2,1)}) custom-call(f32[64,16384]{1,0:T(8,128)} %gu_ref, f32[64,8192]{1,0:T(8,128)} %bitcast.75), custom_call_target="tpu_custom_call" | custom-call | tf_op jit(solution)/shard_map/swap_ffn/pallas_call | solution.py:733
  62.5 3.7 collective-permute-start
  69.1 2.4 collective-permute-done.1
  73.0 43.2 %plane_gather_9.1 = (bf16[8,256,2048]{2,1,0:T(8,128)(2,1)}, f32[8,8,256]{2,1,0:T(8,128)}, f32[8,256,128]{2,1,0:T(8,128)}) custom-call(bf16[256,2048]{1,0:T(8,128)(2,1)} %refs_0_, f32[8,256]{1,0:T(8,128)} %reshape.229.refs_1_, f32[256,128]{1,0:T(8,128)} %select_maximum_fusion.refs_2_), custom_call_target="tpu_custom_call" | custom-call | tf_op jit(solution)/shard_map/plane_gather_9/pallas_call | solution.py:503
  120.8 12.4 %project.1 = (bf16[8,256,2048]{2,1,0:T(8,128)(2,1)}, bf16[2048,256]{1,0:T(8,128)(2,1)}, bf16[2048,128]{1,0:T(8,128)(2,1)}) custom-call(bf16[8,256,2048]{2,1,0:T(8,128)(2,1)} %get-tuple-element.63.x_ref, bf16[2048,640]{1,0:T(8,128)(2,1)} %all-gather.4.cloned.1.call-done.w_ref.refs_2_.refs_3_, f32[1,2048]{1,0:T(1,128)} %slice.44.gain_ref, ...), custom_call_target="tpu_custom_call" | custom-call | tf_op jit(solution)/shard_map/project/pallas_call | solution.py:187
  133.2 81.0 %gather_keys.1 = (bf16[2048,2048]{1,0:T(8,128)(2,1)}, bf16[8,256,2048]{2,1,0:T(8,128)(2,1)}, bf16[4,2048,128]{2,1,0:T(8,128)(2,1)}) custom-call(bf16[2048,640]{1,0:T(8,128)(2,1)} %all-gather.4.cloned.1.call-done.w_ref.refs_2_.refs_3_, bf16[256,2048]{1,0:T(8,128)(2,1)} %dy_ref.1, bf16[2048,128]{1,0:T(8,128)(2,1)} %get-tuple-element.67.kv_ref), custom_call_target="tpu_custom_call" | custom-call | tf_op jit(solution)/shard_map/gather_keys/pallas_call | solution.py:618
  214.3 22.0 %attend.1 = (bf16[2048,256]{1,0:T(8,128)(2,1)}, f32[8,256,4]{2,1,0:T(8,128)}, bf16[256,2048]{1,0:T(8,128)(2,1)}) custom-call(bf16[2048,256]{1,0:T(8,128)(2,1)} %get-tuple-element.66.q_ref, bf16[4,2048,128]{2,1,0:T(8,128)(2,1)} %get-tuple-element.68.kv_ref, f32[8,256,1]{2,1,0:T(8,128)} %copy.44.seg_q_ref, f32[8,1,1024]{2,1,0:T(1,128)} %broadcast_in_dim.45.seg_k_ref), custom_call_target="tpu_custom_call" | custom-call | tf_op jit(solution)/shard_map/attend/pallas_call | solution.py:267
  236.3 6.2 multiply_reduce_fusion.1
  243.7 51.2 %ffn_first.1 = (bf16[8,256,2048]{2,1,0:T(8,128)(2,1)}, bf16[8,256,512]{2,1,0:T(8,128)(2,1)}, bf16[8,256,1024]{2,1,0:T(8,128)(2,1)}) custom-call(bf16[256,2048]{1,0:T(8,128)(2,1)} %multiply_convert_fusion.x_ref, bf16[8,256,2048]{2,1,0:T(8,128)(2,1)} %get-tuple-element.71.dy_ref, bf16[2048,1536]{1,0:T(8,128)(2,1)} %all-gather.6.cloned.1.call-done.w_ref.w_a_ref), custom_call_target="tpu_custom_call" | custom-call | tf_op jit(solution)/shard_map/ffn_first/pallas_call | solution.py:905
  294.9 19.2 %ffn_gradient.2 = bf16[2048,1536]{1,0:T(8,128)(2,1)} custom-call(bf16[8,256,2048]{2,1,0:T(8,128)(2,1)} %get-tuple-element.76.x_ref, bf16[8,256,2048]{2,1,0:T(8,128)(2,1)} %get-tuple-element.71.dy_ref, bf16[8,256,1024]{2,1,0:T(8,128)(2,1)} %get-tuple-element.74.dgu_ref.dgu_a_ref, bf16[8,256,512]{2,1,0:T(8,128)(2,1)} %get-tuple-element.75.hid_ref.hid_a_ref), custom_call_target="tpu_custom_call" | custom-call | tf_op jit(solution)/shard_map/ffn_gradient/pallas_call | solution.py:944
  316.3 16.0 %all-gather.8.cloned.1.call-done.w_ref = bf16[2048,1536]{1,0:T(8,128)(2,1)} async-done(((bf16[512,1536]{1,0:T(8,128)(2,1)}), bf16[2048,1536]{1,0:T(8,128)(2,1)}) %all-gather.8.cloned.1.call-update) | async-done | bytes 6291472 | tf_op jit(solution)/shard_map/all_gather | solution.py:1289
  332.3 92.7 %ffn_second.1 = (bf16[8,256,512]{2,1,0:T(8,128)(2,1)}, bf16[8,256,1024]{2,1,0:T(8,128)(2,1)}, f32[256,2048]{1,0:T(8,128)}, f32[256,2048]{1,0:T(8,128)}) custom-call(bf16[8,256,2048]{2,1,0:T(8,128)(2,1)} %get-tuple-element.76.x_ref, bf16[8,256,2048]{2,1,0:T(8,128)(2,1)} %get-tuple-element.71.dy_ref, bf16[2048,1536]{1,0:T(8,128)(2,1)} %all-gather.8.cloned.1.call-done.w_ref, ...), custom_call_target="tpu_custom_call" | custom-call | tf_op jit(solution)/shard_map/ffn_second/pallas_call | solution.py:1066
  425.1 19.4 %ffn_gradient.3 = bf16[2048,1536]{1,0:T(8,128)(2,1)} custom-call(bf16[8,256,2048]{2,1,0:T(8,128)(2,1)} %get-tuple-element.76.x_ref, bf16[8,256,2048]{2,1,0:T(8,128)(2,1)} %get-tuple-element.71.dy_ref, bf16[8,256,1024]{2,1,0:T(8,128)(2,1)} %get-tuple-element.81.dgu_ref, bf16[8,256,512]{2,1,0:T(8,128)(2,1)} %get-tuple-element.82.hid_ref), custom_call_target="tpu_custom_call" | custom-call | tf_op jit(solution)/shard_map/ffn_gradient/pallas_call | solution.py:944
  445.2 2.8 copy.46.seg_k_ref
  450.5 4.2 fusion.40
  455.6 6.7 convolution_convert_fusion.2.d_ref
  462.3 57.9 %attend_back.1 = (bf16[2048,256]{1,0:T(8,128)(2,1)}, bf16[4,2048,128]{2,1,0:T(8,128)(2,1)}, bf16[8,256,2048]{2,1,0:T(8,128)(2,1)}) custom-call(bf16[256,2048]{1,0:T(8,128)(2,1)} %convolution_convert_fusion.2.d_ref, bf16[2048,256]{1,0:T(8,128)(2,1)} %get-tuple-element.66.q_ref, bf16[4,2048,128]{2,1,0:T(8,128)(2,1)} %get-tuple-element.68.kv_ref, ...), custom_call_target="tpu_custom_call" | custom-call | tf_op jit(solution)/shard_map/attend_back/pallas_call | solution.py:376
  520.2 6.2 convolution_convert_fusion.1
  526.5 2.4 convolution_convert_fusion
  530.4 21.1 %swap_back_13.1 = (bf16[64,16384]{1,0:T(8,128)(2,1)}, bf16[64,8192]{1,0:T(8,128)(2,1)}) custom-call(bf16[8,64,1536]{2,1,0:T(8,128)(2,1)} %bitcast.85), custom_call_target="tpu_custom_call" | custom-call | tf_op jit(solution)/shard_map/swap_back_13/pallas_call | solution.py:789
  551.5 5.5 reduce-scatter.8.cloned.1.call-done
  558.7 21.7 %swap_back_15.1 = (bf16[64,16384]{1,0:T(8,128)(2,1)}, bf16[64,8192]{1,0:T(8,128)(2,1)}) custom-call(bf16[8,64,1536]{2,1,0:T(8,128)(2,1)} %bitcast.86, bf16[64,16384]{1,0:T(8,128)(2,1)} %get-tuple-element.92.refs_1_, bf16[64,8192]{1,0:T(8,128)(2,1)} %get-tuple-element.93.refs_2_), custom_call_target="tpu_custom_call", output_to_operand_aliasing={{0}: (1, {}), {1}: (2, {})} | custom-call | tf_op jit(solution)/shard_map/swap_back_15/pallas_call | solution.py:789
  580.4 12.0 %multiply_subtract_fusion = (f32[64,16384]{1,0:T(8,128)}, f32[64,16384]{1,0:T(8,128)}, f32[64,16384]{1,0:T(8,128)}, f32[64]{0:T(128)S(1)}) fusion(f32[64,16384]{1,0:T(8,128)} %gu_ref, bf16[64,16384]{1,0:T(8,128)(2,1)} %get-tuple-element.95, f32[64,16384]{1,0:T(8,128)} %param.31, f32[64,16384]{1,0:T(8,128)} %param.30), kind=kLoop, calls=%fused_computation.9 | loop fusion | flops 20971456 | bytes 27263232 | tf_op jit(solution)/shard_map/sub | solution.py:78
  592.4 11.1 %reduce-scatter.10.cloned.1.call-done = bf16[1,2048,128]{2,1,0:T(8,128)(2,1)} async-done(((bf16[4,2048,128]{2,1,0:T(8,128)(2,1)}), bf16[1,2048,128]{2,1,0:T(8,128)(2,1)}) %reduce-scatter.10.cloned.1.call-update) | async-done | bytes 524304 | tf_op jit(solution)/shard_map/reduce_scatter | solution.py:1380
  603.8 6.3 multiply_subtract_fusion.1
  613.2 6.8 convolution_convert_fusion.3
  621.2 47.2 %product_sum_6.1 = f32[256,2048]{1,0:T(8,128)} custom-call(bf16[8,256,256]{2,1,0:T(8,128)(2,1)} %bitcast.87, bf16[8,256,128]{2,1,0:T(8,128)(2,1)} %pad_maximum_fusion.1.refs_1_, bf16[2048,640]{1,0:T(8,128)(2,1)} %all-gather.4.cloned.1.call-done.w_ref.refs_2_.refs_3_, bf16[2048,640]{1,0:T(8,128)(2,1)} %all-gather.4.cloned.1.call-done.w_ref.refs_2_.refs_3_), custom_call_target="tpu_custom_call" | custom-call | tf_op jit(solution)/shard_map/product_sum_6/pallas_call | solution.py:1233
  668.4 2.2 fusion.4
  674.4 11.7 %swap_back_14.1 = (bf16[64,2048]{1,0:T(8,128)(2,1)}, bf16[64,1024]{1,0:T(8,128)(2,1)}, bf16[64,2048]{1,0:T(8,128)(2,1)}) custom-call(bf16[8,64,512]{2,1,0:T(8,128)(2,1)} %bitcast.80, bf16[8,64,128]{2,1,0:T(8,128)(2,1)} %bitcast.92), custom_call_target="tpu_custom_call" | custom-call | tf_op jit(solution)/shard_map/swap_back_14/pallas_call | solution.py:789
  687.6 2.8 multiply_subtract_fusion.3
  690.4 2.9 multiply_subtract_fusion.2
  (123 shorter events, 30.3 us)
Async XLA Ops:
  7.2 113.7 %all-gather.4.cloned.1.call-start = ((), (), s32[]{:S(2)}) async-start(), calls=%async_computation.5 | async-start | bytes 3276800 | tf_op jit(solution)/shard_map/all_gather | solution.py:1289
  21.3 222.4 %all-gather.6.cloned.1.call-start = ((), (), s32[]{:S(2)}) async-start(), calls=%async_computation.6 | async-start | bytes 7864320 | tf_op jit(solution)/shard_map/all_gather | solution.py:1289
  21.4 41.1 %copy-start.15 = (f32[2,64]{1,0:T(2,128)S(1)}, f32[2,64]{1,0:T(2,128)}, u32[]{:S(2)}) copy-start(f32[2,64]{1,0:T(2,128)} %param.35) | copy-start | bytes 1540
  21.4 45.8 %copy-start.19 = (s32[256]{0:T(256)S(1)}, s32[256]{0:T(256)}, u32[]{:S(2)}) copy-start(s32[256]{0:T(256)} %param.22) | copy-start | bytes 3076
  62.4 6.6 copy-start.16
  62.5 269.9 %all-gather.8.cloned.1.call-start = ((), (), s32[]{:S(2)}) async-start(), calls=%async_computation.7 | async-start | bytes 7864320 | tf_op jit(solution)/shard_map/all_gather | solution.py:1289
  62.5 6.5 collective-permute-start
  66.2 5.3 collective-permute-start.1
  66.2 5.5 collective-permute-start.2
  116.2 346.1 %reduce-scatter.6.cloned.1.call-start = ((), (), s32[]{:S(2)}) async-start(), calls=%async_computation.8 | async-start | bytes 7864320 | tf_op jit(solution)/shard_map/reduce_scatter | solution.py:1295
  214.3 22.0 %copy-start.2 = (bf16[256,2048]{1,0:T(8,128)(2,1)S(1)}, bf16[256,2048]{1,0:T(8,128)(2,1)}, u32[]{:S(2)}) copy-start(bf16[256,2048]{1,0:T(8,128)(2,1)} %refs_0_) | copy-start | bytes 3145732
  314.1 242.8 %reduce-scatter.8.cloned.1.call-start = ((), (), s32[]{:S(2)}) async-start(), calls=%async_computation.9 | async-start | bytes 7864320 | tf_op jit(solution)/shard_map/reduce_scatter | solution.py:1295
  444.5 159.1 %reduce-scatter.10.cloned.1.call-start = ((), (), s32[]{:S(2)}) async-start(), calls=%async_computation.10 | async-start | bytes 2621440 | tf_op jit(solution)/shard_map/reduce_scatter | solution.py:1380
  448.0 2.2 copy-start.5
  448.0 2.5 copy-start.7
  520.2 6.2 copy-start.20
  520.2 6.4 copy-start.21
  530.4 26.7 %copy-start.1 = (f32[8,256,128]{2,1,0:T(8,128)S(1)}, f32[8,256,128]{2,1,0:T(8,128)}, u32[]{:S(2)}) copy-start(f32[8,256,128]{2,1,0:T(8,128)} %get-tuple-element.65.table_ref) | copy-start | bytes 3145732
  557.0 115.3 %reduce-scatter.12.cloned.1.call-start = ((), (), s32[]{:S(2)}) async-start(), calls=%async_computation.11 | async-start | bytes 2621440 | tf_op jit(solution)/shard_map/reduce_scatter | solution.py:1295
  592.4 11.4 %copy-start.3 = (f32[8192,64]{0,1:T(8,128)S(1)}, f32[8192,64]{0,1:T(8,128)}, u32[]{:S(2)}) copy-start(f32[8192,64]{0,1:T(8,128)} %param.32) | copy-start | bytes 6291460
  603.6 70.9 %reduce-scatter.14.cloned.1.call-start = ((), (), s32[]{:S(2)}) async-start(), calls=%async_computation.12 | async-start | bytes 655360 | tf_op jit(solution)/shard_map/reduce_scatter | solution.py:1295
  603.8 6.3 copy-start.11
  610.5 1.5 copy-start.8
  610.5 1.8 copy-start.9
  621.2 49.5 %copy-start.4 = (f32[256,2048]{1,0:T(8,128)S(1)}, f32[256,2048]{1,0:T(8,128)}, u32[]{:S(2)}) copy-start(f32[256,2048]{1,0:T(8,128)} %get-tuple-element.121) | copy-start | bytes 6291460
  668.4 2.3 copy-start
  672.3 15.3 %copy-start.12 = (f32[2048,64]{0,1:T(8,128)S(1)}, f32[2048,64]{0,1:T(8,128)}, u32[]{:S(2)}) copy-start(f32[2048,64]{0,1:T(8,128)} %param.26) | copy-start | bytes 1572868
  687.3 3.1 copy-start.10
  687.3 3.1 copy-start.13
  687.3 3.1 copy-start.14
  690.4 2.9 copy-start.17
  690.4 2.9 copy-start.18
  (1 other events, 1.0 us)
Sparse Core Ops, SparseCore 0:
  21.5 55.1 all-gather.3
  78.2 120.9 all-gather.5
  200.8 131.4 all-gather.7
  334.5 108.9 reduce-scatter.5
  445.7 111.2 reduce-scatter.7
  559.1 44.3 reduce-scatter.9
  605.9 43.1 reduce-scatter.11
  652.0 20.9 reduce-scatter.13
